TPU v7x, 256 devices: a whole 4x4x8 slice. The times are simulated.
256 devices in a mesh: span: 16 (over x, y), tensor: 16 (over z, core).
Axes of the slice: x: 4, y: 4, z: 8, core: 2. Of those that a mesh axis runs over, the one named last changes fastest.
Arguments:
- tokens: bfloat16 [4096, 4096], P('span', 'tensor'), may hold values from -200 to 200
- retain: float32 [4096], P('span'), may hold values from 0.5 to 1
- norm_gain: float32 [4096], P('tensor'), may hold values from 0.1 to 1.9
- norm_bias: float32 [4096], P('tensor'), may hold values from -2.5 to 2.5
- decay_rate: float32 [16, 4096], P(None, 'tensor'), may hold values from 6.1035156e-05 to 0.0333333333
- ema_angle: float32 [16, 4096], P(None, 'tensor'), may hold values from -0.05 to 0.05
- ema_input: float32 [16, 4096], P(None, 'tensor'), may hold values from -2.4 to 2.4
- ema_output: float32 [2, 16, 4096], P(None, None, 'tensor'), may hold values from -0.25 to 0.25
- ema_skip: float32 [4096], P('tensor'), may hold values from -3 to 3
- shared_weight: bfloat16 [4096, 1024], P('tensor'), may hold values from -0.125 to 0.125
- shared_gain: float32 [1024], replicated, may hold values from 0.1 to 1.9
- output_weight: bfloat16 [1024, 4096], P(None, 'tensor'), may hold values from -0.1875 to 0.1875
Outputs:
- layer_out: bfloat16 [4096, 4096], P('span', 'tensor')
All inputs are finite; a program needn't handle non-finite values.
Results may differ from a plain program's by a relative error of at most 0.02.
Values may be sent and summed in bfloat16 or wider, within the bound.
No kernel may reach another device: no remote copies, remote signals or barrier semaphores. Data moves between devices by JAX's collectives and lax.ppermute only.
A program may use at most 128 MiB of HBM per device.

v0:
```python
import jax
import jax.numpy as jnp
from jax import lax
from jax.sharding import PartitionSpec as P

Z = 1024
GROUP = 64
BLOCK = 64


precise = lax.Precision.HIGHEST
norm_eps = 1e-05
scale_eps = 1e-06


def shifted(shard, axis, by):
    length = lax.axis_size(axis)
    pairs = [(i, i + by) for i in range(length) if 0 <= i + by < length]
    return lax.ppermute(shard, axis, pairs)


def lag_powers(decay_rate, ema_angle, count):
    lag_steps = jnp.arange(count, dtype=jnp.int32).astype(jnp.float32)[:, None, None]
    magnitude = jnp.exp(-decay_rate[None] * lag_steps)
    return (
        magnitude * jnp.cos(ema_angle[None] * lag_steps),
        magnitude * jnp.sin(ema_angle[None] * lag_steps),
    )


def toeplitz(kernel):
    width = kernel.shape[0]
    flipped = jnp.concatenate([kernel[::-1], jnp.zeros_like(kernel)], axis=0)
    repeated = jnp.tile(flipped, (width, 1))[: width * (2 * width - 1)]
    return repeated.reshape(width, 2 * width - 1, kernel.shape[1])[:, width - 1 : 2 * width - 1]


def block_combine(earlier, later):
    mult_re = later[0] * earlier[0] - later[1] * earlier[1]
    mult_im = later[0] * earlier[1] + later[1] * earlier[0]
    add_re = later[0] * earlier[2] - later[1] * earlier[3] + later[2]
    add_im = later[0] * earlier[3] + later[1] * earlier[2] + later[3]
    return (mult_re, mult_im, add_re, add_im)


def group_terms(tokens):
    values = tokens.astype(jnp.float32)
    grouped = values.reshape(values.shape[0], -1, GROUP)
    return (grouped, jnp.sum(grouped, axis=2), jnp.sum(grouped * grouped, axis=2))


def timestep_norm(grouped, group_sums, group_squares, before, first_row, norm_gain, norm_bias):
    length = grouped.shape[0]
    cum_sum = before[0][None] + jnp.cumsum(group_sums, axis=0)
    cum_sq = before[1][None] + jnp.cumsum(group_squares, axis=0)
    counts = ((first_row + jnp.arange(length, dtype=jnp.int32) + 1) * GROUP).astype(jnp.float32)[
        :, None
    ]
    average = cum_sum / counts
    spread = cum_sq / counts - average * average
    inverse = lax.rsqrt(spread + norm_eps)
    normed = (grouped - average[:, :, None]) * inverse[:, :, None]
    return normed.reshape(length, -1) * norm_gain[None] + norm_bias[None]


def ema_local(normed, retain, decay_rate, ema_angle, ema_input, ema_output):
    length, channels = normed.shape
    blocks = length // BLOCK
    power_real, power_im = lag_powers(decay_rate, ema_angle, BLOCK + 1)
    weight = (1.0 - jnp.exp(-decay_rate)) * ema_input
    kernel = jnp.sum(
        weight[None]
        * (ema_output[0][None] * power_real[:BLOCK] - ema_output[1][None] * power_im[:BLOCK]),
        axis=1,
    )
    matrix = toeplitz(kernel)
    retained = jnp.cumprod(retain.reshape(blocks, BLOCK), axis=1)
    scaled = normed.reshape(blocks, BLOCK, channels) / retained[:, :, None]
    within = jnp.einsum("tsd,bsd->btd", matrix, scaled, precision=precise)
    back_re = power_real[:BLOCK][::-1]
    back_im = power_im[:BLOCK][::-1]
    end_re = weight[None] * jnp.einsum("bsd,sjd->bjd", scaled, back_re, precision=precise)
    end_im = weight[None] * jnp.einsum("bsd,sjd->bjd", scaled, back_im, precision=precise)
    closing = retained[:, -1][:, None, None]
    elements = (
        closing * power_real[BLOCK][None],
        closing * power_im[BLOCK][None],
        closing * end_re,
        closing * end_im,
    )
    return (within, retained, elements, (power_real, power_im))


def ema_finish(within, retained, prior_re, prior_im, powers, ema_output, normed, ema_skip):
    power_real, power_im = powers
    multiplier_cosine_part = (
        ema_output[0][None] * power_real[1:] - ema_output[1][None] * power_im[1:]
    )
    coeff_im = ema_output[0][None] * power_im[1:] + ema_output[1][None] * power_real[1:]
    carried_part = jnp.einsum(
        "bjd,tjd->btd", prior_re, multiplier_cosine_part, precision=precise
    ) - jnp.einsum("bjd,tjd->btd", prior_im, coeff_im, precision=precise)
    mixed = retained[:, :, None] * (within + carried_part)
    return mixed.reshape(normed.shape) + ema_skip[None] * normed


def shards(
    tokens,
    retain,
    norm_gain,
    norm_bias,
    decay_rate,
    ema_angle,
    ema_input,
    ema_output,
    ema_skip,
    shared_weight,
    shared_gain,
    output_weight,
):
    length = tokens.shape[0]
    interval_number = lax.axis_size("span")
    grouped, group_sums, group_squares = group_terms(tokens)
    local_stats = jnp.stack([jnp.sum(group_sums, axis=0), jnp.sum(group_squares, axis=0)])

    def stat_turn(turn_index, carried):
        return shifted(carried + local_stats, "span", 1)

    before = lax.fori_loop(0, interval_number - 1, stat_turn, jnp.zeros_like(local_stats))
    first_row = lax.axis_index("span") * length
    normed = timestep_norm(
        grouped, group_sums, group_squares, before, first_row, norm_gain, norm_bias
    )
    within, retained, elements, powers = ema_local(
        normed, retain, decay_rate, ema_angle, ema_input, ema_output
    )
    inclusive = lax.associative_scan(block_combine, elements)
    summary = tuple((member[-1] for member in inclusive))

    def state_turn(turn_index, carried):
        moved_re = summary[0] * carried[0] - summary[1] * carried[1] + summary[2]
        moved_im = summary[0] * carried[1] + summary[1] * carried[0] + summary[3]
        return shifted(jnp.stack([moved_re, moved_im]).astype(jnp.bfloat16), "span", 1).astype(
            jnp.float32
        )

    incoming_state = lax.fori_loop(
        0, interval_number - 1, state_turn, jnp.zeros((2,) + summary[0].shape, jnp.float32)
    )
    state_re = incoming_state[0]
    state_im = incoming_state[1]
    mult_re = jnp.concatenate([jnp.ones_like(inclusive[0][:1]), inclusive[0][:-1]], axis=0)
    mult_im = jnp.concatenate([jnp.zeros_like(inclusive[1][:1]), inclusive[1][:-1]], axis=0)
    local_re = jnp.concatenate([jnp.zeros_like(inclusive[2][:1]), inclusive[2][:-1]], axis=0)
    local_im = jnp.concatenate([jnp.zeros_like(inclusive[3][:1]), inclusive[3][:-1]], axis=0)
    prior_re = mult_re * state_re[None] - mult_im * state_im[None] + local_re
    prior_im = mult_re * state_im[None] + mult_im * state_re[None] + local_im
    ema = ema_finish(within, retained, prior_re, prior_im, powers, ema_output, normed, ema_skip)
    active = jax.nn.silu(ema).astype(jnp.bfloat16)
    tensor_count = lax.axis_size("tensor")
    shared_rows = Z // tensor_count
    shared_part = lax.psum_scatter(
        lax.dot_general(
            shared_weight, active, (((0,), (1,)), ((), ())), preferred_element_type=jnp.float32
        ).astype(jnp.bfloat16),
        "tensor",
        scatter_dimension=0,
        tiled=True,
    ).astype(jnp.float32)
    part_squares = jnp.sum(shared_part * shared_part, axis=0)
    total_squares = lax.psum(part_squares, "tensor")
    inverse = lax.rsqrt(total_squares / Z + scale_eps)
    gain_part = lax.dynamic_slice_in_dim(
        shared_gain, lax.axis_index("tensor") * shared_rows, shared_rows, 0
    )
    common_rescaled = (shared_part * inverse[None, :] * gain_part[:, None]).astype(jnp.bfloat16)
    mixed = lax.dot_general(
        lax.all_gather(common_rescaled, "tensor", axis=0, tiled=True),
        output_weight,
        (((0,), (0,)), ((), ())),
        preferred_element_type=jnp.float32,
    )
    return mixed.astype(jnp.bfloat16)


def solution(mesh):
    in_specs = (
        P("span", "tensor"),
        P("span"),
        P("tensor"),
        P("tensor"),
        P(None, "tensor"),
        P(None, "tensor"),
        P(None, "tensor"),
        P(None, None, "tensor"),
        P("tensor"),
        P("tensor", None),
        P(),
        P(None, "tensor"),
    )
    out_specs = P("span", "tensor")
    return jax.shard_map(shards, mesh=mesh, in_specs=in_specs, out_specs=out_specs, check_vma=False)
```

profile of v0, /device:TPU:1, one launch (start us, length us, event | category | flops | bytes accessed | tf_op | source)
XLA Modules:
  0.0 1123.9 jit_solution(12982040948489419083)
XLA Ops:
  18.9 6.2 slice.215
  40.5 86.3 %while.21 = (s32[]{:T(128)}, f32[2,4]{1,0:T(2,128)S(1)}, f32[2,4]{1,0:T(2,128)S(1)}, s32[]{:T(128)}) while((s32[]{:T(128)}, f32[2,4]{1,0:T(2,128)S(1)}, f32[2,4]{1,0:T(2,128)S(1)}, s32[]{:T(128)}) %tuple.84), condition=%wide.region_6.0_spmd, body=%wide.region_5.0_spmd.sunk | while | flops 10 | bytes 317 | solution.py:129
  182.4 76.6 %pad.71 = f32[4,16,256]{1,0,2:T(4,128)} pad(f32[2,16,256]{1,0,2:T(2,128)S(1)} %copy.170, f32[]{:T(128)} %constant.22.clone.1), padding=0_1_1x0_0_0x0_0_0 | pad | bytes 98308 | tf_op jit(solution)/shard_map/pad | solution.py:137
  259.8 76.7 %pad.91 = f32[3,16,256]{1,0,2:T(4,128)} pad(f32[2,16,256]{1,0,2:T(2,128)S(1)} %copy.157, f32[]{:T(128)} %constant.22.clone.1), padding=0_0_1x0_0_0x0_0_0 | pad | bytes 81924 | tf_op jit(solution)/shard_map/slice | solution.py:153
  336.5 76.9 %pad.63 = f32[4,16,256]{1,0,2:T(4,128)} pad(f32[2,16,256]{1,0,2:T(2,128)S(1)} %copy.157, f32[]{:T(128)} %constant.22.clone.1), padding=0_1_1x0_0_0x0_0_0 | pad | bytes 98308 | tf_op jit(solution)/shard_map/pad | solution.py:137
  413.9 76.7 %pad.93 = f32[3,16,256]{1,0,2:T(4,128)} pad(f32[2,16,256]{1,0,2:T(2,128)S(1)} %copy.165, f32[]{:T(128)} %constant.22.clone.1), padding=0_0_1x0_0_0x0_0_0 | pad | bytes 81924 | tf_op jit(solution)/shard_map/slice | solution.py:154
  490.6 76.5 %pad.69 = f32[4,16,256]{1,0,2:T(4,128)} pad(f32[2,16,256]{1,0,2:T(2,128)S(1)} %copy.165, f32[]{:T(128)} %constant.22.clone.1), padding=0_1_1x0_0_0x0_0_0 | pad | bytes 98308 | tf_op jit(solution)/shard_map/pad | solution.py:137
  567.1 76.6 %pad.144 = f32[3,16,256]{1,0,2:T(4,128)} pad(f32[2,16,256]{1,0,2:T(2,128)S(1)} %pad_add_fusion.3, f32[]{:T(128)} %constant.22.clone.1), padding=0_0_1x0_0_0x0_0_0 | pad | bytes 81924
  643.7 76.5 %pad.62 = f32[4,16,256]{1,0,2:T(4,128)} pad(f32[2,16,256]{1,0,2:T(2,128)S(1)} %pad_add_fusion.3, f32[]{:T(128)} %constant.22.clone.1), padding=1_0_1x0_0_0x0_0_0 | pad | bytes 98308 | tf_op jit(solution)/shard_map/pad | solution.py:137
  730.9 76.7 %pad.61 = f32[4,16,256]{1,0,2:T(4,128)} pad(f32[2,16,256]{1,0,2:T(2,128)S(1)} %copy.153, f32[]{:T(128)} %constant.22.clone.1), padding=0_1_1x0_0_0x0_0_0 | pad | bytes 98308 | tf_op jit(solution)/shard_map/pad | solution.py:137
  816.0 99.6 %while.22 = (s32[]{:T(128)}, f32[2,16,256]{2,1,0:T(8,128)S(1)}, f32[16,256]{1,0:T(8,128)S(1)}, f32[16,256]{1,0:T(8,128)S(1)}, f32[16,256]{1,0:T(8,128)S(1)}, /*index=5*/f32[16,256]{1,0:T(8,128)S(1)}, s32[]{:T(128)}, s32[]{:T(128)}) while((s32[]{:T(128)}, f32[2,16,256]{2,1,0:T(8,128)S(1)}, f32[16,256]{1,0:T(8,128)S(1)}, ...), condition=%wide.region_15.16_spmd.clone, body=%wide.region_14.15_spmd.clone.sunk | while | flops 65539 | bytes 327815 | solution.py:147
  822.7 5.8 collective-permute-start.1
  842.6 5.7 collective-permute-start.1
  849.3 5.7 collective-permute-start.1
  855.9 5.7 collective-permute-start.1
  862.5 5.7 collective-permute-start.1
  869.2 5.7 collective-permute-start.1
  895.7 5.7 collective-permute-start.1
  926.1 7.2 reshape.89
  938.3 9.3 copy.184
  956.1 13.4 %fusion.6 = f32[4,64,256]{1,0,2:T(4,128)S(1)} fusion(f32[4,64,256]{1,0,2:T(4,128)S(1)} %fusion.11, f32[64,64,256]{1,0,2:T(8,128)S(1)} %copy-done.1, f32[4,64]{1,0:T(4,128)S(1)} %copy-done.29, f32[4,64,256]{1,0,2:T(4,128)S(1)} %copy-done.8), kind=kOutput, calls=%fused_computation.20 | convolution fusion | flops 50528256 | bytes 4981760 | tf_op jit(solution)/shard_map/tsd,bsd->btd/dot_general | solution.py:79
  972.1 98.6 %reduce-scatter.4.cloned.1.call-done = bf16[64,256]{1,0:T(8,128)(2,1)} async-done(((bf16[1024,256]{1,0:T(8,128)(2,1)}), bf16[64,256]{1,0:T(8,128)(2,1)}) %reduce-scatter.4.cloned.1.call-update) | async-done | bytes 32784 | tf_op jit(solution)/shard_map/reduce_scatter | solution.py:162
  1071.5 26.5 %psum.7 = f32[256]{0:T(256)S(1)} all-reduce(f32[256]{0:T(256)S(1)} %fusion.43), channel_id=1, replica_groups=mesh['span'=16,'tensor'=16] {'tensor'}, use_global_device_ids=true, to_apply=%region_18.19 | all-reduce | flops 256 | bytes 2048 | tf_op jit(solution)/shard_map/psum | solution.py:171
  1098.8 17.0 %all_gather.3 = bf16[1024,256]{1,0:T(8,128)(2,1)S(1)} all-gather(bf16[64,256]{1,0:T(8,128)(2,1)S(1)} %fusion.45), channel_id=1, replica_groups=mesh['span'=16,'tensor'=16] {'tensor'}, dimensions={0}, use_global_device_ids=true | all-gather | bytes 557056 | tf_op jit(solution)/shard_map/all_gather | solution.py:178
  (330 shorter events, 277.5 us)
Async XLA Ops:
  6.5 1064.2 %reduce-scatter.4.cloned.1.call-start = ((), (), s32[]{:S(2)}) async-start(), calls=%async_computation.1 | async-start | bytes 557056 | tf_op jit(solution)/shard_map/reduce_scatter | solution.py:162
  62.7 6.4 collective-permute-start
  69.2 6.4 collective-permute-start
  75.6 6.4 collective-permute-start
  82.0 6.4 collective-permute-start
  88.4 6.4 collective-permute-start
  107.6 6.4 collective-permute-start
  114.1 6.4 collective-permute-start
  120.5 6.4 collective-permute-start
  816.1 6.6 collective-permute-start.1
  822.7 6.7 collective-permute-start.1
  829.4 6.6 collective-permute-start.1
  836.0 6.6 collective-permute-start.1
  842.6 6.6 collective-permute-start.1
  849.3 6.6 collective-permute-start.1
  855.9 6.6 collective-permute-start.1
  862.5 6.6 collective-permute-start.1
  869.2 6.6 collective-permute-start.1
  875.8 6.6 collective-permute-start.1
  882.5 6.6 collective-permute-start.1
  889.1 6.6 collective-permute-start.1
  895.7 6.6 collective-permute-start.1
  902.4 6.6 collective-permute-start.1
  909.0 6.6 collective-permute-start.1
  (40 other events, 3349.0 us)
Sparse Core Ops, SparseCore 0:
  971.4 99.2 reduce-scatter.3
where the time goes:
time: 1130 us; the launch traced here: 1120 us
  local copies, waits for them, and re-layouts  712 us (63%)
  starting transfers between devices  162 us (14%)
  waiting for transfers between devices  122 us (11%)
  blocking collectives  43.4 us (4%)
  other arithmetic  37.8 us (3%)
  matrix products  32 us (3%)
  between operations  14.2 us (1%)
    pad x6, local copies, waits for them, and re-layouts, shards(): inclusive = lax.associative_scan(block_combine, elements)  387 us
    ppermute x30, starting transfers between devices, shifted(): return lax.ppermute(shard, axis, pairs)  162 us
    reduce_scatter x1, waiting for transfers between devices, shards(): lax.psum_scatter(lax.dot_general(shared_weight, active, (((0,), (1,)), ((...  98.6 us
    unnamed x82, local copies, waits for them, and re-layouts  95.6 us
    slice x1, local copies, waits for them, and re-layouts, shards(): inclusive[1][:-1]  76.7 us
    slice x1, local copies, waits for them, and re-layouts, shards(): inclusive[2][:-1]  76.7 us
    slice x13, local copies, waits for them, and re-layouts, shards(): inclusive = lax.associative_scan(block_combine, elements)  30.3 us
    psum x1, blocking collectives, shards(): total_squares = lax.psum(part_squares, 'tensor')  26.5 us
  transfers between devices with their start and end apart: 31, of which 31 were waited for; matrix products, arithmetic and copies ran while one was open for 0% of the time, Pallas kernels for 0%

commit v1 on v0

v1 whole, which is shorter than its diff:
```python
import functools

import jax
import jax.numpy as jnp
from jax import lax
from jax.experimental import pallas as pl
from jax.experimental.pallas import tpu as pltpu
from jax.sharding import PartitionSpec as P

GROUP = 64
SPANS = 16
LENGTH = 256
WIDTH = 256
NDIM = 16
BLOCKS = 8
STEPS = 32
HALF = 128
CHUNK = 8

norm_eps = 1e-05
scale_eps = 1e-06

f32 = jnp.float32
bf16 = jnp.bfloat16
VMEM = pl.BlockSpec(memory_space=pltpu.VMEM)


def dot(a, b):
    return lax.dot_general(a, b, (((1,), (0,)), ((), ())), preferred_element_type=f32)


def iota2(shape, axis):
    return lax.broadcasted_iota(jnp.int32, shape, axis)


def time_of(row):
    return (row % BLOCKS) * STEPS + row // BLOCKS


def as_bf16(mask):
    return jnp.where(mask, 1.0, 0.0).astype(bf16)


def dot_parts(a, b):
    high = a.astype(bf16)
    rest = a - high.astype(f32)
    middle = rest.astype(bf16)
    low = (rest - middle.astype(f32)).astype(bf16)
    return dot(high, b) + dot(middle, b) + dot(low, b)


def cmul(ar, ai, br, bi):
    return ar * br - ai * bi, ar * bi + ai * br


def stats_kernel(tokens_ref, retain_ref, out_ref):
    values = tokens_ref[...].astype(f32)
    total = jnp.sum(values, axis=0, keepdims=True)
    squares = jnp.sum(values * values, axis=0, keepdims=True)
    kept = retain_ref[...]
    size = LENGTH
    while size > 1:
        size //= 2
        kept = kept[:, :size] * kept[:, size:]
    row = iota2((8, WIDTH), 0)
    block = jnp.where(row == 0, total, jnp.where(row == 1, squares, kept))
    for i in range(SPANS):
        out_ref[8 * i : 8 * i + 8, :] = block


def local_kernel(
    tokens_ref,
    stats_ref,
    retain_ref,
    gain_ref,
    bias_ref,
    decay_ref,
    angle_ref,
    input_ref,
    output_ref,
    message_ref,
    scaled_ref,
    retained_ref,
    state_ref,
    pack_ref,
    summary,
):
    me = lax.axis_index("span")
    before = jnp.zeros((8, WIDTH), f32)
    for i in range(SPANS):
        before += jnp.where(i < me, stats_ref[8 * i : 8 * i + 8, :], 0.0)

    tokens = tokens_ref[...]
    row = time_of(iota2((LENGTH, LENGTH), 0))
    column = iota2((LENGTH, LENGTH), 1)
    upto = as_bf16(column <= row)
    groups = as_bf16(iota2((WIDTH, WIDTH), 0) // GROUP == iota2((WIDTH, WIDTH), 1) // GROUP)
    values = tokens.astype(f32)
    squares = values * values
    high = squares.astype(bf16)
    low = (squares - high.astype(f32)).astype(bf16)
    cum_sum = dot_parts(dot(upto, tokens) + before[0:1], groups)
    cum_sq = dot_parts(dot(upto, high) + dot(upto, low) + before[1:2], groups)
    placed = dot(as_bf16(column == row), tokens)
    position = time_of(iota2((LENGTH, WIDTH), 0)) + me * LENGTH + 1
    share = 1.0 / (position * GROUP).astype(f32)
    average = cum_sum * share
    spread = cum_sq * share - average * average
    inverse = lax.rsqrt(spread + norm_eps)
    normed = (placed - average) * inverse * gain_ref[...] + bias_ref[...]

    factor = jnp.sum(jnp.where(column == row, retain_ref[...], 0.0), axis=1, keepdims=True)
    running = jnp.ones((BLOCKS, HALF), f32)
    for step in range(STEPS):
        rows = slice(BLOCKS * step, BLOCKS * step + BLOCKS)
        running = running * factor[rows]
        retained_ref[rows, :] = running
        back = 1.0 / running
        for h in range(2):
            lanes = slice(HALF * h, HALF * h + HALF)
            scaled_ref[rows, lanes] = normed[rows, lanes] * back

    decay = decay_ref[...]
    size = jnp.exp(-decay)
    power_re = size * jnp.cos(angle_ref[...])
    power_im = size * jnp.sin(angle_ref[...])
    weight = (1.0 - size) * input_ref[...]
    pack_ref[0:16, :] = power_re
    pack_ref[16:32, :] = power_im
    pack_ref[32:48, :] = output_ref[0] * weight
    pack_ref[48:64, :] = output_ref[1] * weight
    at_re, at_im = power_re, power_im
    for k in range(1, 9):
        at_re, at_im = cmul(at_re, at_im, at_re, at_im)
        if k >= 5:
            place = 64 + 32 * (k - 5)
            pack_ref[place : place + 16, :] = at_re
            pack_ref[place + 16 : place + 32, :] = at_im

    block = iota2((BLOCKS, HALF), 0)
    spans = [running]
    for k in range(2):
        reach = spans[-1]
        shifted = jnp.where(block >= 2**k, pltpu.roll(reach, 2**k, 0), 1.0)
        spans.append(reach * shifted)
    spans = [jnp.where(block >= 2**k, spans[k], 0.0) for k in range(3)]

    def wide(place, lanes):
        return jnp.broadcast_to(pack_ref[place : place + 1, lanes], (BLOCKS, HALF))

    for h in range(2):
        lanes = slice(HALF * h, HALF * h + HALF)
        for first in range(0, NDIM, CHUNK):
            js = range(first, first + CHUNK)
            re_of = [wide(j, lanes) for j in js]
            im_of = [wide(16 + j, lanes) for j in js]

            def step_on(step, held):
                u = scaled_ref[pl.ds(pl.multiple_of(step * BLOCKS, BLOCKS), BLOCKS), lanes]
                following = []
                for n in range(CHUNK):
                    re, im = held[2 * n], held[2 * n + 1]
                    following.append(re * re_of[n] - im * im_of[n] + u)
                    following.append(re * im_of[n] + im * re_of[n])
                return tuple(following)

            u0 = scaled_ref[0:BLOCKS, lanes]
            u1 = scaled_ref[BLOCKS : 2 * BLOCKS, lanes]
            begin = []
            for n in range(CHUNK):
                begin += [u0 * re_of[n] + u1, u0 * im_of[n]]
            ends = lax.fori_loop(2, STEPS, step_on, tuple(begin), unroll=3)
            for n, j in enumerate(js):
                re, im = running * ends[2 * n], running * ends[2 * n + 1]
                for k in range(3):
                    add_re, add_im = cmul(
                        pltpu.roll(re, 2**k, 0),
                        pltpu.roll(im, 2**k, 0),
                        wide(64 + 32 * k + j, lanes),
                        wide(80 + 32 * k + j, lanes),
                    )
                    re, im = re + spans[k] * add_re, im + spans[k] * add_im
                summary[j : j + 1, lanes] = re[7:8]
                summary[16 + j : 17 + j, lanes] = im[7:8]
                place = (h * NDIM + j) * 16
                state_ref[place : place + 8, :] = jnp.where(block >= 1, pltpu.roll(re, 1, 0), 0.0)
                state_ref[place + 8 : place + 16, :] = jnp.where(
                    block >= 1, pltpu.roll(im, 1, 0), 0.0
                )
    sent = summary[...].astype(bf16)
    for i in range(SPANS):
        message_ref[32 * i : 32 * i + 32, :] = sent


def finish_kernel(
    message_ref,
    stats_ref,
    scaled_ref,
    retained_ref,
    state_ref,
    pack_ref,
    skip_ref,
    weight_ref,
    give_ref,
    keep_ref,
    entering,
    mixed,
):
    me = lax.axis_index("span")
    core = lax.axis_index("tensor") % 2
    far_re, far_im = pack_ref[160:176, :], pack_ref[176:192, :]

    def turn(i, held):
        kept = stats_ref[pl.ds(i * 8 + 2, 1), :]
        piece = message_ref[pl.ds(pl.multiple_of(i * 32, 32), 32), :].astype(f32)
        re, im = cmul(held[0], held[1], far_re, far_im)
        return re * kept + piece[:16], im * kept + piece[16:]

    start = jnp.zeros((NDIM, WIDTH), f32)
    state_re, state_im = lax.fori_loop(0, me, turn, (start, start))
    entering[0:16, :] = state_re
    entering[16:32, :] = state_im

    block = iota2((BLOCKS, HALF), 0)
    closing = retained_ref[LENGTH - BLOCKS : LENGTH, :]
    ahead = jnp.where(block >= 1, pltpu.roll(closing, 1, 0), 1.0)
    for k in range(3):
        ahead = ahead * jnp.where(block >= 2**k, pltpu.roll(ahead, 2**k, 0), 1.0)

    def wide(ref, place, lanes):
        return jnp.broadcast_to(ref[place : place + 1, lanes], (BLOCKS, HALF))

    for h in range(2):
        lanes = slice(HALF * h, HALF * h + HALF)
        for first in range(0, NDIM, CHUNK):
            js = range(first, first + CHUNK)
            begin = []
            for j in js:
                re = ahead * wide(entering, j, lanes)
                im = ahead * wide(entering, 16 + j, lanes)
                for k in range(3):
                    on_re, on_im = cmul(
                        re,
                        im,
                        wide(pack_ref, 64 + 32 * k + j, lanes),
                        wide(pack_ref, 80 + 32 * k + j, lanes),
                    )
                    chosen = (block // 2**k) % 2 == 1
                    re, im = jnp.where(chosen, on_re, re), jnp.where(chosen, on_im, im)
                place = (h * NDIM + j) * 16
                begin.append(re + state_ref[place : place + 8, :])
                begin.append(im + state_ref[place + 8 : place + 16, :])
            re_of = [wide(pack_ref, j, lanes) for j in js]
            im_of = [wide(pack_ref, 16 + j, lanes) for j in js]
            out_re = [wide(pack_ref, 32 + j, lanes) for j in js]
            out_im = [wide(pack_ref, 48 + j, lanes) for j in js]
            skip = jnp.broadcast_to(skip_ref[:, lanes], (BLOCKS, HALF))

            def step_on(step, held):
                rows = pl.ds(pl.multiple_of(step * BLOCKS, BLOCKS), BLOCKS)
                u = scaled_ref[rows, lanes]
                following = []
                terms = []
                for n in range(CHUNK):
                    re, im = held[2 * n], held[2 * n + 1]
                    next_re = re * re_of[n] - im * im_of[n] + u
                    next_im = re * im_of[n] + im * re_of[n]
                    following += [next_re, next_im]
                    terms.append(out_re[n] * next_re - out_im[n] * next_im)
                while len(terms) > 1:
                    terms = [terms[i] + terms[i + 1] for i in range(0, len(terms), 2)]
                if first == 0:
                    mixed[rows, lanes] = terms[0] + skip * u
                else:
                    mixed[rows, lanes] += terms[0]
                return tuple(following)

            lax.fori_loop(0, STEPS, step_on, tuple(begin), unroll=2)

    retained = retained_ref[...]
    ema = jnp.concatenate([retained, retained], axis=1) * mixed[...]
    active = (ema / (1.0 + jnp.exp(-ema))).astype(bf16)
    slot = iota2((LENGTH, LENGTH), 0)
    side = jnp.where(slot < HALF, 1 - core, core)
    within = slot % HALF
    wanted = (within // 16) * 32 + side * 16 + within % 16
    chosen = as_bf16(time_of(iota2((LENGTH, LENGTH), 1)) == wanted)
    ordered = dot(chosen, active).astype(bf16)
    product = dot(ordered, weight_ref[...]).astype(bf16)
    give_ref[...] = product[:HALF]
    keep_ref[...] = product[HALF:]


def norm_kernel(parts_ref, gain_ref, out_ref):
    total = parts_ref[0:16, :].astype(f32)
    for i in range(1, 8):
        total += parts_ref[16 * i : 16 * i + 16, :].astype(f32)
    squares = jnp.mean(total * total, axis=1, keepdims=True)
    out_ref[...] = (total * lax.rsqrt(squares + scale_eps) * gain_ref[...]).astype(bf16)


def call(kernel, count, shapes, scratch=()):
    single = len(shapes) == 1
    made = [jax.ShapeDtypeStruct(s, d) for s, d in shapes]
    return pl.pallas_call(
        kernel,
        out_shape=made[0] if single else made,
        in_specs=[VMEM] * count,
        out_specs=VMEM if single else [VMEM] * len(shapes),
        scratch_shapes=list(scratch),
        compiler_params=pltpu.CompilerParams(vmem_limit_bytes=32 * 2**20),
    )


def shards(
    tokens,
    retain,
    norm_gain,
    norm_bias,
    decay_rate,
    ema_angle,
    ema_input,
    ema_output,
    ema_skip,
    shared_weight,
    shared_gain,
    output_weight,
):
    retain = retain.reshape(1, LENGTH)
    with jax.named_scope("stats"):
        own = call(stats_kernel, 2, [((8 * SPANS, WIDTH), f32)])(tokens, retain)
        stats = lax.all_to_all(own, "span", 0, 0, tiled=True)
    with jax.named_scope("local"):
        message, scaled, retained, state, pack = call(
            local_kernel,
            9,
            [
                ((32 * SPANS, WIDTH), bf16),
                ((LENGTH, WIDTH), f32),
                ((LENGTH, HALF), f32),
                ((2 * NDIM * 16, HALF), f32),
                ((192, WIDTH), f32),
            ],
            [pltpu.VMEM((32, WIDTH), f32)],
        )(
            tokens,
            stats,
            retain,
            norm_gain.reshape(1, WIDTH),
            norm_bias.reshape(1, WIDTH),
            decay_rate,
            ema_angle,
            ema_input,
            ema_output,
        )
        message = lax.all_to_all(message, "span", 0, 0, tiled=True)
    with jax.named_scope("finish"):
        width = shared_weight.shape[1]
        give, keep = call(
            finish_kernel,
            8,
            [((HALF, width), bf16), ((HALF, width), bf16)],
            [pltpu.VMEM((32, WIDTH), f32), pltpu.VMEM((LENGTH, WIDTH), f32)],
        )(
            message,
            stats,
            scaled,
            retained,
            state,
            pack,
            ema_skip.reshape(1, WIDTH),
            shared_weight,
        )
    with jax.named_scope("shared"):
        taken = lax.ppermute(give, "tensor", [(i, i ^ 1) for i in range(16)])
        pair = (taken.astype(f32) + keep.astype(f32)).astype(bf16)
        groups = [[core + 2 * z for z in range(8)] for core in range(2)]
        parts = lax.all_to_all(pair, "tensor", 0, 0, tiled=True, axis_index_groups=groups)
        normed = call(norm_kernel, 2, [((16, width), bf16)])(parts, shared_gain.reshape(1, width))
    with jax.named_scope("output"):
        whole = lax.all_gather(normed, "tensor", axis=0, tiled=True)
        return lax.dot_general(
            whole, output_weight, (((1,), (0,)), ((), ())), preferred_element_type=f32
        ).astype(bf16)


def solution(mesh):
    in_specs = (
        P("span", "tensor"),
        P("span"),
        P("tensor"),
        P("tensor"),
        P(None, "tensor"),
        P(None, "tensor"),
        P(None, "tensor"),
        P(None, None, "tensor"),
        P("tensor"),
        P("tensor", None),
        P(),
        P(None, "tensor"),
    )
    out_specs = P("span", "tensor")
    return jax.shard_map(shards, mesh=mesh, in_specs=in_specs, out_specs=out_specs, check_vma=False)
```

time: 1130 us -> 75.1 us (0.07)
  local copies, waits for them, and re-layouts: 712 us -> 2.36 us
  starting transfers between devices: 162 us -> 3.28 us
  waiting for transfers between devices: 122 us -> 1.16 us
  other arithmetic: 37.8 us -> 0.07 us
  matrix products: 32 us -> 0.96 us
  blocking collectives: 43.4 us -> 61.8 us
  between operations: 14.2 us -> 0.1 us
    pad x6 -> x0, local copies, waits for them, and re-layouts: 387 us -> none  [shards(): inclusive = lax.associative_scan(block_combine, elements)]
    slice x22 -> x0, local copies, waits for them, and re-layouts: 198 us -> none  [the longest x1 76.7 us: shards(): inclusive[1][:-1]]
    ppermute x30 -> x1, starting transfers between devices: 162 us -> 3.28 us  [shards(): taken = lax.ppermute(give, 'tensor', [(i, i ^ 1) for i in range(16)])]
    reduce_scatter x1 -> x0, waiting for transfers between devices: 98.6 us -> none  [shards(): lax.psum_scatter(lax.dot_general(shared_weight, active, (((0,), (1,)), ((...]
    unnamed x82 -> x24, local copies, waits for them, and re-layouts: 95.6 us -> 2.36 us
    all_to_all x0 -> x3, blocking collectives: none -> 44.1 us  [the longest x1 19.1 us: shards(): lax.all_to_all(pair, 'tensor', 0, 0, tiled=True, axis_index_groups=groups)]
    dot_general x7 -> x1, matrix products: 32 us -> 0.96 us  [shards(): lax.dot_general(whole, output_weight, (((1,), (0,)), ((), ())), preferred...]
    psum x1 -> x0, blocking collectives: 26.5 us -> none  [shards(): total_squares = lax.psum(part_squares, 'tensor')]
  transfers between devices with their start and end apart: 31 -> 1, of which waited for: 31 -> 1; matrix products, arithmetic and copies ran while one was open for 0% -> 0% of each run, Pallas kernels for 0% -> 0%
where the time goes in v1:
time: 75.1 us; the launch traced here: 74.8 us
  blocking collectives  61.8 us (82%)
  Pallas kernels  5.15 us (7%)
  starting transfers between devices  3.28 us (4%)
  local copies, waits for them, and re-layouts  2.36 us (3%)
  waiting for transfers between devices  1.16 us (2%)
  matrix products  0.96 us (1%)
    all_to_all x1, blocking collectives, shards(): lax.all_to_all(pair, 'tensor', 0, 0, tiled=True, axis_index_groups=groups)  19.1 us
    all_gather x1, blocking collectives, shards(): whole = lax.all_gather(normed, 'tensor', axis=0, tiled=True)  17.7 us
    all_to_all x1, blocking collectives, shards(): stats = lax.all_to_all(own, 'span', 0, 0, tiled=True)  14.4 us
    all_to_all x1, blocking collectives, shards(): message = lax.all_to_all(message, 'span', 0, 0, tiled=True)  10.6 us
    ppermute x1, starting transfers between devices, shards(): taken = lax.ppermute(give, 'tensor', [(i, i ^ 1) for i in range(16)])  3.28 us
    pallas_call x1, Pallas kernels, shards(): call(finish_kernel, 8, [((HALF, width), bf16), ((HALF, width), bf16)], [p...  2.55 us
    unnamed x24, local copies, waits for them, and re-layouts  2.36 us
    pallas_call x1, Pallas kernels, shards(): call(local_kernel, 9, [((32 * SPANS, WIDTH), bf16), ((LENGTH, WIDTH), f32...  1.92 us
  transfers between devices with their start and end apart: 1, of which 1 were waited for; matrix products, arithmetic and copies ran while one was open for 0% of the time, Pallas kernels for 0%

profile of v1, /device:TPU:1, one launch (start us, length us, event | category | flops | bytes accessed | tf_op | source)
XLA Modules:
  0.0 74.8 jit_solution(18363515058996437701)
XLA Ops:
  0.0 0.0 copy-start
  0.0 0.7 copy-done.8
  0.7 0.9 %copy-done.2 = bf16[256,256]{1,0:T(8,128)(2,1)S(1)} copy-done((bf16[256,256]{1,0:T(8,128)(2,1)S(1)}, bf16[256,256]{1,0:T(8,128)(2,1)}, u32[]{:S(2)}) %copy-start.2) | copy-done | bytes 131096
  1.7 0.0 copy-start.9
  1.7 0.0 copy-start.10
  1.7 0.6 stats.1
  2.2 0.0 copy-start.1
  2.3 14.4 %all_to_all.33 = f32[16,8,256]{2,1,0:T(8,128)S(1)} all-to-all(f32[16,8,256]{2,1,0:T(8,128)S(1)} %bitcast.17), channel_id=1, replica_groups=mesh['span'=16,'tensor'=16] {'span'}, dimensions={0} | all-to-all | bytes 262144 | tf_op jit(solution)/shard_map/stats/all_to_all | solution.py:332
  16.6 0.0 copy-done.3
  16.6 0.0 copy-done.6
  16.7 0.0 copy-done.9
  16.7 0.0 copy-done.10
  16.7 1.9 %local.1 = (bf16[512,256]{1,0:T(8,128)(2,1)S(1)}, f32[256,256]{1,0:T(8,128)S(1)}, f32[256,128]{1,0:T(8,128)S(1)}, f32[512,128]{1,0:T(8,128)S(1)}, f32[192,256]{1,0:T(8,128)S(1)}) custom-call(bf16[256,256]{1,0:T(8,128)(2,1)S(1)} %copy-done.2, f32[128,256]{1,0:T(8,128)S(1)} %bitcast.13, f32[1,256]{1,0:T(1,128)S(1)} %bitcast.21, f32[1,256]{1,0:T(1,128)S(1)} %bitcast.22, ...), custom_call_target="tpu_custom_call" | custom-call | tf_op jit(solution)/shard_map/local/pallas_call | solution.py:334
  18.6 10.6 %all_to_all.34 = bf16[16,32,256]{2,1,0:T(8,128)(2,1)S(1)} all-to-all(bf16[16,32,256]{2,1,0:T(8,128)(2,1)S(1)} %bitcast.18), channel_id=1, replica_groups=mesh['span'=16,'tensor'=16] {'span'}, dimensions={0} | all-to-all | bytes 524288 | tf_op jit(solution)/shard_map/local/all_to_all | solution.py:356
  29.2 0.7 copy-done.11
  29.9 2.6 %finish.1 = (bf16[128,1024]{1,0:T(8,128)(2,1)S(1)}, bf16[128,1024]{1,0:T(8,128)(2,1)S(1)}) custom-call(bf16[512,256]{1,0:T(8,128)(2,1)S(1)} %bitcast.16, f32[128,256]{1,0:T(8,128)S(1)} %bitcast.14, f32[256,256]{1,0:T(8,128)S(1)} %get-tuple-element.13.scaled_ref, f32[256,128]{1,0:T(8,128)S(1)} %get-tuple-element.14.retained_ref, ...), custom_call_target="tpu_custom_call" | custom-call | tf_op jit(solution)/shard_map/finish/pallas_call | solution.py:359
  32.4 3.3 %collective-permute-start = (bf16[128,1024]{1,0:T(8,128)(2,1)S(1)}, bf16[128,1024]{1,0:T(8,128)(2,1)S(1)}, u32[]{:S(2)}, u32[]{:S(2)}) collective-permute-start(bf16[128,1024]{1,0:T(8,128)(2,1)S(1)} %get-tuple-element.17), channel_id=1, source_target_pairs={{0,1},{1,0},{2,3},{3,2},{4,5},{5,4},{6,7},{7,6},{8,9},{9,8},{10,11... | collective-permute-start | bytes 786440 | tf_op jit(solution)/shard_map/shared/ppermute | solution.py:375
  35.7 1.2 %collective-permute-done = bf16[128,1024]{1,0:T(8,128)(2,1)S(1)} collective-permute-done((bf16[128,1024]{1,0:T(8,128)(2,1)S(1)}, bf16[128,1024]{1,0:T(8,128)(2,1)S(1)}, u32[]{:S(2)}, u32[]{:S(2)}) %collective-permute-start) | collective-permute-done | bytes 262176 | tf_op jit(solution)/shard_map/shared/ppermute | solution.py:375
  36.9 0.1 add_convert_fusion
  37.0 0.0 copy-start.7
  37.0 19.1 %all_to_all.35 = bf16[8,16,1024]{2,1,0:T(8,128)(2,1)S(1)} all-to-all(bf16[8,16,1024]{2,1,0:T(8,128)(2,1)S(1)} %bitcast.25), channel_id=1, replica_groups={{0,2,4,6,8,10,12,14},{1,3,5,7,9,11,13,15},{16,18,20,22,24,26,28,30},{17..., dimensions={0} | all-to-all | bytes 524288 | tf_op jit(solution)/shard_map/shared/all_to_all | solution.py:378
  56.0 0.1 shared.1
  56.2 17.7 %all_gather.3 = bf16[256,1024]{1,0:T(8,128)(2,1)S(1)} all-gather(bf16[16,1024]{1,0:T(8,128)(2,1)S(1)} %shared.1), channel_id=1, replica_groups=mesh['span'=16,'tensor'=16] {'tensor'}, dimensions={0}, use_global_device_ids=true | all-gather | bytes 557056 | tf_op jit(solution)/shard_map/output/all_gather | solution.py:381
  73.9 1.0 %convolution_convert_fusion = bf16[256,256]{1,0:T(8,128)(2,1)} fusion(bf16[256,1024]{1,0:T(8,128)(2,1)S(1)} %all_gather.3, bf16[1024,256]{1,0:T(8,128)(2,1)S(1)} %copy-done), kind=kOutput, calls=%fused_computation | convolution fusion | flops 134283264 | bytes 1179648 | tf_op jit(solution)/shard_map/output/dot_general | solution.py:382
  (12 shorter events, 0.0 us)
Async XLA Ops:
  0.0 73.9 %copy-start = (bf16[1024,256]{1,0:T(8,128)(2,1)S(1)}, bf16[1024,256]{1,0:T(8,128)(2,1)}, u32[]{:S(2)}) copy-start(bf16[1024,256]{1,0:T(8,128)(2,1)} %param.23) | copy-start | bytes 1572868
  0.0 0.7 copy-start.8
  0.7 0.9 %copy-start.2 = (bf16[256,256]{1,0:T(8,128)(2,1)S(1)}, bf16[256,256]{1,0:T(8,128)(2,1)}, u32[]{:S(2)}) copy-start(bf16[256,256]{1,0:T(8,128)(2,1)} %tokens_ref.3) | copy-start | bytes 393220
  1.6 15.0 %copy-start.3 = (f32[2,16,256]{2,1,0:T(8,128)S(1)}, f32[2,16,256]{2,1,0:T(8,128)}, u32[]{:S(2)}) copy-start(f32[2,16,256]{2,1,0:T(8,128)} %output_ref.1) | copy-start | bytes 98308
  1.6 15.0 %copy-start.4 = (f32[16,256]{1,0:T(8,128)S(1)}, f32[16,256]{1,0:T(8,128)}, u32[]{:S(2)}) copy-start(f32[16,256]{1,0:T(8,128)} %decay_ref.1) | copy-start | bytes 49156
  1.6 15.0 %copy-start.5 = (f32[16,256]{1,0:T(8,128)S(1)}, f32[16,256]{1,0:T(8,128)}, u32[]{:S(2)}) copy-start(f32[16,256]{1,0:T(8,128)} %angle_ref.1) | copy-start | bytes 49156
  1.7 15.0 %copy-start.6 = (f32[16,256]{1,0:T(8,128)S(1)}, f32[16,256]{1,0:T(8,128)}, u32[]{:S(2)}) copy-start(f32[16,256]{1,0:T(8,128)} %input_ref.1) | copy-start | bytes 49156
  1.7 15.0 %copy-start.9 = (f32[256]{0:T(256)S(1)}, f32[256]{0:T(256)}, u32[]{:S(2)}) copy-start(f32[256]{0:T(256)} %param.14) | copy-start | bytes 3076
  1.7 15.0 %copy-start.10 = (f32[256]{0:T(256)S(1)}, f32[256]{0:T(256)}, u32[]{:S(2)}) copy-start(f32[256]{0:T(256)} %param.15) | copy-start | bytes 3076
  2.2 27.0 %copy-start.1 = (bf16[256,1024]{1,0:T(8,128)(2,1)S(1)}, bf16[256,1024]{1,0:T(8,128)(2,1)}, u32[]{:S(2)}) copy-start(bf16[256,1024]{1,0:T(8,128)(2,1)} %weight_ref.1) | copy-start | bytes 1572868
  29.2 0.7 copy-start.11
  32.4 4.4 %collective-permute-start = (bf16[128,1024]{1,0:T(8,128)(2,1)S(1)}, bf16[128,1024]{1,0:T(8,128)(2,1)S(1)}, u32[]{:S(2)}, u32[]{:S(2)}) collective-permute-start(bf16[128,1024]{1,0:T(8,128)(2,1)S(1)} %get-tuple-element.17), channel_id=1, source_target_pairs={{0,1},{1,0},{2,3},{3,2},{4,5},{5,4},{6,7},{7,6},{8,9},{9,8},{10,11... | collective-permute-start | bytes 786440 | tf_op jit(solution)/shard_map/shared/ppermute | solution.py:375
  37.0 19.1 %copy-start.7 = (f32[1024]{0:T(1024)S(1)}, f32[1024]{0:T(1024)}, u32[]{:S(2)}) copy-start(f32[1024]{0:T(1024)} %param.22) | copy-start | bytes 12292

commit v2 on v1

--- a/solution.py
+++ b/solution.py
@@ -53,7 +53,15 @@
     return ar * br - ai * bi, ar * bi + ai * br
 
 
-def stats_kernel(tokens_ref, retain_ref, out_ref):
+def stats_kernel(tokens_hbm, retain_hbm, out_ref, tokens_ref, retain_ref, arrived):
+    copies = (
+        pltpu.make_async_copy(tokens_hbm, tokens_ref, arrived.at[0]),
+        pltpu.make_async_copy(retain_hbm, retain_ref, arrived.at[1]),
+    )
+    for copy in copies:
+        copy.start()
+    for copy in copies:
+        copy.wait()
     values = tokens_ref[...].astype(f32)
     total = jnp.sum(values, axis=0, keepdims=True)
     squares = jnp.sum(values * values, axis=0, keepdims=True)
@@ -78,6 +86,7 @@
     angle_ref,
     input_ref,
     output_ref,
+    skip_ref,
     message_ref,
     scaled_ref,
     retained_ref,
@@ -129,6 +138,7 @@
     pack_ref[16:32, :] = power_im
     pack_ref[32:48, :] = output_ref[0] * weight
     pack_ref[48:64, :] = output_ref[1] * weight
+    pack_ref[192:200, :] = jnp.broadcast_to(skip_ref[...], (8, WIDTH))
     at_re, at_im = power_re, power_im
     for k in range(1, 9):
         at_re, at_im = cmul(at_re, at_im, at_re, at_im)
@@ -199,7 +209,6 @@
     retained_ref,
     state_ref,
     pack_ref,
-    skip_ref,
     weight_ref,
     give_ref,
     keep_ref,
@@ -254,7 +263,7 @@
             im_of = [wide(pack_ref, 16 + j, lanes) for j in js]
             out_re = [wide(pack_ref, 32 + j, lanes) for j in js]
             out_im = [wide(pack_ref, 48 + j, lanes) for j in js]
-            skip = jnp.broadcast_to(skip_ref[:, lanes], (BLOCKS, HALF))
+            skip = pack_ref[192:200, lanes]
 
             def step_on(step, held):
                 rows = pl.ds(pl.multiple_of(step * BLOCKS, BLOCKS), BLOCKS)
@@ -281,9 +290,7 @@
     ema = jnp.concatenate([retained, retained], axis=1) * mixed[...]
     active = (ema / (1.0 + jnp.exp(-ema))).astype(bf16)
     slot = iota2((LENGTH, LENGTH), 0)
-    side = jnp.where(slot < HALF, 1 - core, core)
-    within = slot % HALF
-    wanted = (within // 16) * 32 + side * 16 + within % 16
+    wanted = (slot + (1 - core) * HALF) % LENGTH
     chosen = as_bf16(time_of(iota2((LENGTH, LENGTH), 1)) == wanted)
     ordered = dot(chosen, active).astype(bf16)
     product = dot(ordered, weight_ref[...]).astype(bf16)
@@ -296,19 +303,25 @@
     for i in range(1, 8):
         total += parts_ref[16 * i : 16 * i + 16, :].astype(f32)
     squares = jnp.mean(total * total, axis=1, keepdims=True)
-    out_ref[...] = (total * lax.rsqrt(squares + scale_eps) * gain_ref[...]).astype(bf16)
-
-
-def call(kernel, count, shapes, scratch=()):
+    normed = (total * lax.rsqrt(squares + scale_eps) * gain_ref[...]).astype(bf16)
+    for i in range(8):
+        out_ref[16 * i : 16 * i + 16, :] = normed
+
+
+def output_kernel(shared_ref, weight_ref, out_ref):
+    out_ref[...] = dot(shared_ref[...], weight_ref[...]).astype(bf16)
+
+
+def call(kernel, count, shapes, scratch=(), space=VMEM, limit=32):
     single = len(shapes) == 1
     made = [jax.ShapeDtypeStruct(s, d) for s, d in shapes]
     return pl.pallas_call(
         kernel,
         out_shape=made[0] if single else made,
-        in_specs=[VMEM] * count,
+        in_specs=[space] * count,
         out_specs=VMEM if single else [VMEM] * len(shapes),
         scratch_shapes=list(scratch),
-        compiler_params=pltpu.CompilerParams(vmem_limit_bytes=32 * 2**20),
+        compiler_params=pltpu.CompilerParams(vmem_limit_bytes=limit * 2**20),
     )
 
 
@@ -328,18 +341,29 @@
 ):
     retain = retain.reshape(1, LENGTH)
     with jax.named_scope("stats"):
-        own = call(stats_kernel, 2, [((8 * SPANS, WIDTH), f32)])(tokens, retain)
+        own = call(
+            stats_kernel,
+            2,
+            [((8 * SPANS, WIDTH), f32)],
+            [
+                pltpu.VMEM((LENGTH, WIDTH), bf16),
+                pltpu.VMEM((1, LENGTH), f32),
+                pltpu.SemaphoreType.DMA((2,)),
+            ],
+            pl.BlockSpec(memory_space=pltpu.HBM),
+            60,
+        )(tokens, retain)
         stats = lax.all_to_all(own, "span", 0, 0, tiled=True)
     with jax.named_scope("local"):
         message, scaled, retained, state, pack = call(
             local_kernel,
-            9,
+            10,
             [
                 ((32 * SPANS, WIDTH), bf16),
                 ((LENGTH, WIDTH), f32),
                 ((LENGTH, HALF), f32),
                 ((2 * NDIM * 16, HALF), f32),
-                ((192, WIDTH), f32),
+                ((200, WIDTH), f32),
             ],
             [pltpu.VMEM((32, WIDTH), f32)],
         )(
@@ -352,13 +376,14 @@
             ema_angle,
             ema_input,
             ema_output,
+            ema_skip.reshape(1, WIDTH),
         )
         message = lax.all_to_all(message, "span", 0, 0, tiled=True)
     with jax.named_scope("finish"):
         width = shared_weight.shape[1]
         give, keep = call(
             finish_kernel,
-            8,
+            7,
             [((HALF, width), bf16), ((HALF, width), bf16)],
             [pltpu.VMEM((32, WIDTH), f32), pltpu.VMEM((LENGTH, WIDTH), f32)],
         )(
@@ -368,7 +393,6 @@
             retained,
             state,
             pack,
-            ema_skip.reshape(1, WIDTH),
             shared_weight,
         )
     with jax.named_scope("shared"):
@@ -376,12 +400,12 @@
         pair = (taken.astype(f32) + keep.astype(f32)).astype(bf16)
         groups = [[core + 2 * z for z in range(8)] for core in range(2)]
         parts = lax.all_to_all(pair, "tensor", 0, 0, tiled=True, axis_index_groups=groups)
-        normed = call(norm_kernel, 2, [((16, width), bf16)])(parts, shared_gain.reshape(1, width))
+        copies = call(norm_kernel, 2, [((HALF, width), bf16)])(parts, shared_gain.reshape(1, width))
     with jax.named_scope("output"):
-        whole = lax.all_gather(normed, "tensor", axis=0, tiled=True)
-        return lax.dot_general(
-            whole, output_weight, (((1,), (0,)), ((), ())), preferred_element_type=f32
-        ).astype(bf16)
+        half = lax.all_to_all(copies, "tensor", 0, 0, tiled=True, axis_index_groups=groups)
+        pairs = [[2 * z, 2 * z + 1] for z in range(8)]
+        whole = lax.all_gather(half, "tensor", axis=0, tiled=True, axis_index_groups=pairs)
+        return call(output_kernel, 2, [((LENGTH, WIDTH), bf16)])(whole, output_weight)
 
 
 def solution(mesh):

time: 75.1 us -> 74.3 us (0.989)
  Pallas kernels: 5.15 us -> 7.8 us
  local copies, waits for them, and re-layouts: 2.36 us -> 0.05 us
  matrix products: 0.96 us -> 0 us
    all_gather x1, blocking collectives: 17.7 us -> 5.1 us  [shards(): lax.all_gather(half, 'tensor', axis=0, tiled=True, axis_index_groups=pairs)]
    all_to_all x0 -> x1, blocking collectives: none -> 12.1 us  [shards(): lax.all_to_all(copies, 'tensor', 0, 0, tiled=True, axis_index_groups=groups)]
    pallas_call x4 -> x5, Pallas kernels: 5.15 us -> 7.8 us  [the longest x1 2.55 us: shards(): call(finish_kernel, 7, [((HALF, width), bf16), ((HALF, width), bf16)], [p...]
    unnamed x24, local copies, waits for them, and re-layouts: 2.36 us -> 0.05 us
    dot_general x1 -> x0, matrix products: 0.96 us -> none  [shards(): lax.dot_general(whole, output_weight, (((1,), (0,)), ((), ())), preferred...]
where the time goes in v2:
time: 74.3 us; the launch traced here: 74 us
  blocking collectives  61.4 us (83%)
  Pallas kernels  7.8 us (10%)
  starting transfers between devices  3.28 us (4%)
  waiting for transfers between devices  1.16 us (2%)
    all_to_all x1, blocking collectives, shards(): lax.all_to_all(pair, 'tensor', 0, 0, tiled=True, axis_index_groups=groups)  19.1 us
    all_to_all x1, blocking collectives, shards(): stats = lax.all_to_all(own, 'span', 0, 0, tiled=True)  14.6 us
    all_to_all x1, blocking collectives, shards(): lax.all_to_all(copies, 'tensor', 0, 0, tiled=True, axis_index_groups=groups)  12.1 us
    all_to_all x1, blocking collectives, shards(): message = lax.all_to_all(message, 'span', 0, 0, tiled=True)  10.6 us
    all_gather x1, blocking collectives, shards(): lax.all_gather(half, 'tensor', axis=0, tiled=True, axis_index_groups=pairs)  5.1 us
    ppermute x1, starting transfers between devices, shards(): taken = lax.ppermute(give, 'tensor', [(i, i ^ 1) for i in range(16)])  3.28 us
    pallas_call x1, Pallas kernels, shards(): call(finish_kernel, 7, [((HALF, width), bf16), ((HALF, width), bf16)], [p...  2.55 us
    pallas_call x1, Pallas kernels, shards(): call(stats_kernel, 2, [((8 * SPANS, WIDTH), f32)], [pltpu.VMEM((LENGTH, W...  2.24 us
  transfers between devices with their start and end apart: 1, of which 1 were waited for; matrix products, arithmetic and copies ran while one was open for 0% of the time, Pallas kernels for 0%

profile of v2, /device:TPU:1, one launch (start us, length us, event | category | flops | bytes accessed | tf_op | source)
XLA Modules:
  0.0 74.0 jit_solution(4551312522671359407)
XLA Ops:
  0.0 0.0 copy-start.5
  0.0 0.0 copy-start.6
  0.0 0.0 copy-start.8
  0.0 0.0 copy-start.9
  0.0 0.0 copy-start.10
  0.1 2.2 %stats.1 = f32[128,256]{1,0:T(8,128)} custom-call(bf16[256,256]{1,0:T(8,128)(2,1)} %tokens_ref.1, f32[1,256]{1,0:T(1,128)} %bitcast.20), custom_call_target="tpu_custom_call" | custom-call | tf_op jit(solution)/shard_map/stats/pallas_call | solution.py:344
  2.3 0.0 copy-start
  2.3 14.6 %all_to_all.45 = f32[16,8,256]{2,1,0:T(8,128)S(1)} all-to-all(f32[16,8,256]{2,1,0:T(8,128)} %bitcast.27), channel_id=1, replica_groups=mesh['span'=16,'tensor'=16] {'span'}, dimensions={0} | all-to-all | bytes 262144 | tf_op jit(solution)/shard_map/stats/all_to_all | solution.py:356
  16.9 0.0 copy-done.2
  16.9 0.0 copy-done.4
  17.0 1.9 %local.1 = (bf16[512,256]{1,0:T(8,128)(2,1)S(1)}, f32[256,256]{1,0:T(8,128)S(1)}, f32[256,128]{1,0:T(8,128)S(1)}, f32[512,128]{1,0:T(8,128)S(1)}, f32[200,256]{1,0:T(8,128)S(1)}) custom-call(bf16[256,256]{1,0:T(8,128)(2,1)S(1)} %copy-done.2, f32[128,256]{1,0:T(8,128)S(1)} %bitcast.13, f32[1,256]{1,0:T(1,128)S(1)} %bitcast.21, f32[1,256]{1,0:T(1,128)S(1)} %bitcast.22, ...), custom_call_target="tpu_custom_call" | custom-call | tf_op jit(solution)/shard_map/local/pallas_call | solution.py:358
  18.9 10.6 %all_to_all.46 = bf16[16,32,256]{2,1,0:T(8,128)(2,1)S(1)} all-to-all(bf16[16,32,256]{2,1,0:T(8,128)(2,1)S(1)} %bitcast.18), channel_id=1, replica_groups=mesh['span'=16,'tensor'=16] {'span'}, dimensions={0} | all-to-all | bytes 524288 | tf_op jit(solution)/shard_map/local/all_to_all | solution.py:381
  29.5 0.0 copy-done
  29.5 2.6 %finish.1 = (bf16[128,1024]{1,0:T(8,128)(2,1)S(1)}, bf16[128,1024]{1,0:T(8,128)(2,1)S(1)}) custom-call(bf16[512,256]{1,0:T(8,128)(2,1)S(1)} %bitcast.15, f32[128,256]{1,0:T(8,128)S(1)} %bitcast.14, f32[256,256]{1,0:T(8,128)S(1)} %get-tuple-element.13.scaled_ref, f32[256,128]{1,0:T(8,128)S(1)} %get-tuple-element.14.retained_ref, ...), custom_call_target="tpu_custom_call" | custom-call | tf_op jit(solution)/shard_map/finish/pallas_call | solution.py:384
  32.1 3.3 %collective-permute-start = (bf16[128,1024]{1,0:T(8,128)(2,1)S(1)}, bf16[128,1024]{1,0:T(8,128)(2,1)S(1)}, u32[]{:S(2)}, u32[]{:S(2)}) collective-permute-start(bf16[128,1024]{1,0:T(8,128)(2,1)S(1)} %get-tuple-element.17), channel_id=1, source_target_pairs={{0,1},{1,0},{2,3},{3,2},{4,5},{5,4},{6,7},{7,6},{8,9},{9,8},{10,11... | collective-permute-start | bytes 786440 | tf_op jit(solution)/shard_map/shared/ppermute | solution.py:399
  35.4 1.2 %collective-permute-done = bf16[128,1024]{1,0:T(8,128)(2,1)S(1)} collective-permute-done((bf16[128,1024]{1,0:T(8,128)(2,1)S(1)}, bf16[128,1024]{1,0:T(8,128)(2,1)S(1)}, u32[]{:S(2)}, u32[]{:S(2)}) %collective-permute-start) | collective-permute-done | bytes 262176 | tf_op jit(solution)/shard_map/shared/ppermute | solution.py:399
  36.5 0.1 add_convert_fusion
  36.6 0.0 copy-start.7
  36.6 19.1 %all_to_all.47 = bf16[8,16,1024]{2,1,0:T(8,128)(2,1)S(1)} all-to-all(bf16[8,16,1024]{2,1,0:T(8,128)(2,1)S(1)} %bitcast.25), channel_id=1, replica_groups={{0,2,4,6,8,10,12,14},{1,3,5,7,9,11,13,15},{16,18,20,22,24,26,28,30},{17..., dimensions={0} | all-to-all | bytes 524288 | tf_op jit(solution)/shard_map/shared/all_to_all | solution.py:402
  55.7 0.1 shared.1
  55.8 12.1 %all_to_all.48 = bf16[8,16,1024]{2,1,0:T(8,128)(2,1)S(1)} all-to-all(bf16[8,16,1024]{2,1,0:T(8,128)(2,1)S(1)} %bitcast.17), channel_id=1, replica_groups={{0,2,4,6,8,10,12,14},{1,3,5,7,9,11,13,15},{16,18,20,22,24,26,28,30},{17..., dimensions={0} | all-to-all | bytes 524288 | tf_op jit(solution)/shard_map/output/all_to_all | solution.py:405
  67.9 5.1 %all_gather.3.shared_ref = bf16[256,1024]{1,0:T(8,128)(2,1)S(1)} all-gather(bf16[128,1024]{1,0:T(8,128)(2,1)S(1)} %bitcast.26), channel_id=1, replica_groups={{0,1},{2,3},{4,5},{6,7},{8,9},{10,11},{12,13},{14,15},{16,17},{18,19},{..., dimensions={0}, use_global_device_ids=true | all-gather | bytes 786432 | tf_op jit(solution)/shard_map/output/all_gather | solution.py:407
  73.0 0.0 copy-done.1
  73.0 1.0 %output.1 = bf16[256,256]{1,0:T(8,128)(2,1)} custom-call(bf16[256,1024]{1,0:T(8,128)(2,1)S(1)} %all_gather.3.shared_ref, bf16[1024,256]{1,0:T(8,128)(2,1)S(1)} %copy-done.1), custom_call_target="tpu_custom_call" | custom-call | tf_op jit(solution)/shard_map/output/pallas_call | solution.py:408
  (13 shorter events, 0.0 us)
Async XLA Ops:
  0.0 16.9 %copy-start.2 = (bf16[256,256]{1,0:T(8,128)(2,1)S(1)}, bf16[256,256]{1,0:T(8,128)(2,1)}, u32[]{:S(2)}) copy-start(bf16[256,256]{1,0:T(8,128)(2,1)} %tokens_ref.1) | copy-start | bytes 393220
  0.0 16.9 %copy-start.3 = (f32[2,16,256]{2,1,0:T(8,128)S(1)}, f32[2,16,256]{2,1,0:T(8,128)}, u32[]{:S(2)}) copy-start(f32[2,16,256]{2,1,0:T(8,128)} %output_ref.1) | copy-start | bytes 98308
  0.0 16.9 %copy-start.4 = (f32[16,256]{1,0:T(8,128)S(1)}, f32[16,256]{1,0:T(8,128)}, u32[]{:S(2)}) copy-start(f32[16,256]{1,0:T(8,128)} %decay_ref.1) | copy-start | bytes 49156
  0.0 16.9 %copy-start.5 = (f32[16,256]{1,0:T(8,128)S(1)}, f32[16,256]{1,0:T(8,128)}, u32[]{:S(2)}) copy-start(f32[16,256]{1,0:T(8,128)} %angle_ref.1) | copy-start | bytes 49156
  0.0 16.9 %copy-start.6 = (f32[16,256]{1,0:T(8,128)S(1)}, f32[16,256]{1,0:T(8,128)}, u32[]{:S(2)}) copy-start(f32[16,256]{1,0:T(8,128)} %input_ref.1) | copy-start | bytes 49156
  0.0 16.9 %copy-start.8 = (f32[256]{0:T(256)S(1)}, f32[256]{0:T(256)}, u32[]{:S(2)}) copy-start(f32[256]{0:T(256)} %param.13) | copy-start | bytes 3076
  0.0 16.9 %copy-start.9 = (f32[256]{0:T(256)S(1)}, f32[256]{0:T(256)}, u32[]{:S(2)}) copy-start(f32[256]{0:T(256)} %param.14) | copy-start | bytes 3076
  0.0 16.9 %copy-start.10 = (f32[256]{0:T(256)S(1)}, f32[256]{0:T(256)}, u32[]{:S(2)}) copy-start(f32[256]{0:T(256)} %param.15) | copy-start | bytes 3076
  0.1 16.9 %copy-start.11 = (f32[256]{0:T(256)S(1)}, f32[256]{0:T(256)}, u32[]{:S(2)}) copy-start(f32[256]{0:T(256)} %param.20) | copy-start | bytes 3076
  2.3 27.2 %copy-start = (bf16[256,1024]{1,0:T(8,128)(2,1)S(1)}, bf16[256,1024]{1,0:T(8,128)(2,1)}, u32[]{:S(2)}) copy-start(bf16[256,1024]{1,0:T(8,128)(2,1)} %weight_ref.2) | copy-start | bytes 1572868
  32.1 4.4 %collective-permute-start = (bf16[128,1024]{1,0:T(8,128)(2,1)S(1)}, bf16[128,1024]{1,0:T(8,128)(2,1)S(1)}, u32[]{:S(2)}, u32[]{:S(2)}) collective-permute-start(bf16[128,1024]{1,0:T(8,128)(2,1)S(1)} %get-tuple-element.17), channel_id=1, source_target_pairs={{0,1},{1,0},{2,3},{3,2},{4,5},{5,4},{6,7},{7,6},{8,9},{9,8},{10,11... | collective-permute-start | bytes 786440 | tf_op jit(solution)/shard_map/shared/ppermute | solution.py:399
  36.6 19.1 %copy-start.7 = (f32[1024]{0:T(1024)S(1)}, f32[1024]{0:T(1024)}, u32[]{:S(2)}) copy-start(f32[1024]{0:T(1024)} %param.22) | copy-start | bytes 12292
  67.9 5.1 %copy-start.1 = (bf16[1024,256]{1,0:T(8,128)(2,1)S(1)}, bf16[1024,256]{1,0:T(8,128)(2,1)}, u32[]{:S(2)}) copy-start(bf16[1024,256]{1,0:T(8,128)(2,1)} %weight_ref.3) | copy-start | bytes 1572868

commit v3 on v2

--- a/solution.py
+++ b/solution.py
@@ -76,47 +76,32 @@
         out_ref[8 * i : 8 * i + 8, :] = block
 
 
-def local_kernel(
+def prepare_kernel(
     tokens_ref,
-    stats_ref,
     retain_ref,
-    gain_ref,
-    bias_ref,
     decay_ref,
     angle_ref,
     input_ref,
     output_ref,
     skip_ref,
-    message_ref,
-    scaled_ref,
+    sums_ref,
+    squares_ref,
+    placed_ref,
     retained_ref,
-    state_ref,
+    back_ref,
     pack_ref,
-    summary,
 ):
-    me = lax.axis_index("span")
-    before = jnp.zeros((8, WIDTH), f32)
-    for i in range(SPANS):
-        before += jnp.where(i < me, stats_ref[8 * i : 8 * i + 8, :], 0.0)
-
     tokens = tokens_ref[...]
     row = time_of(iota2((LENGTH, LENGTH), 0))
     column = iota2((LENGTH, LENGTH), 1)
     upto = as_bf16(column <= row)
-    groups = as_bf16(iota2((WIDTH, WIDTH), 0) // GROUP == iota2((WIDTH, WIDTH), 1) // GROUP)
     values = tokens.astype(f32)
     squares = values * values
     high = squares.astype(bf16)
     low = (squares - high.astype(f32)).astype(bf16)
-    cum_sum = dot_parts(dot(upto, tokens) + before[0:1], groups)
-    cum_sq = dot_parts(dot(upto, high) + dot(upto, low) + before[1:2], groups)
-    placed = dot(as_bf16(column == row), tokens)
-    position = time_of(iota2((LENGTH, WIDTH), 0)) + me * LENGTH + 1
-    share = 1.0 / (position * GROUP).astype(f32)
-    average = cum_sum * share
-    spread = cum_sq * share - average * average
-    inverse = lax.rsqrt(spread + norm_eps)
-    normed = (placed - average) * inverse * gain_ref[...] + bias_ref[...]
+    sums_ref[...] = dot(upto, tokens)
+    squares_ref[...] = dot(upto, high) + dot(upto, low)
+    placed_ref[...] = dot(as_bf16(column == row), tokens)
 
     factor = jnp.sum(jnp.where(column == row, retain_ref[...], 0.0), axis=1, keepdims=True)
     running = jnp.ones((BLOCKS, HALF), f32)
@@ -124,10 +109,7 @@
         rows = slice(BLOCKS * step, BLOCKS * step + BLOCKS)
         running = running * factor[rows]
         retained_ref[rows, :] = running
-        back = 1.0 / running
-        for h in range(2):
-            lanes = slice(HALF * h, HALF * h + HALF)
-            scaled_ref[rows, lanes] = normed[rows, lanes] * back
+        back_ref[rows, :] = 1.0 / running
 
     decay = decay_ref[...]
     size = jnp.exp(-decay)
@@ -146,6 +128,39 @@
             place = 64 + 32 * (k - 5)
             pack_ref[place : place + 16, :] = at_re
             pack_ref[place + 16 : place + 32, :] = at_im
+
+def local_kernel(
+    stats_ref,
+    sums_ref,
+    squares_ref,
+    placed_ref,
+    retained_ref,
+    back_ref,
+    pack_ref,
+    gain_ref,
+    bias_ref,
+    message_ref,
+    scaled_ref,
+    state_ref,
+    summary,
+):
+    me = lax.axis_index("span")
+    before = jnp.zeros((8, WIDTH), f32)
+    for i in range(SPANS):
+        before += jnp.where(i < me, stats_ref[8 * i : 8 * i + 8, :], 0.0)
+
+    groups = as_bf16(iota2((WIDTH, WIDTH), 0) // GROUP == iota2((WIDTH, WIDTH), 1) // GROUP)
+    cum_sum = dot_parts(sums_ref[...] + before[0:1], groups)
+    cum_sq = dot_parts(squares_ref[...] + before[1:2], groups)
+    position = time_of(iota2((LENGTH, WIDTH), 0)) + me * LENGTH + 1
+    share = 1.0 / (position * GROUP).astype(f32)
+    average = cum_sum * share
+    spread = cum_sq * share - average * average
+    inverse = lax.rsqrt(spread + norm_eps)
+    normed = (placed_ref[...] - average) * inverse * gain_ref[...] + bias_ref[...]
+    back = back_ref[...]
+    scaled_ref[...] = normed * jnp.concatenate([back, back], axis=1)
+    running = retained_ref[LENGTH - BLOCKS : LENGTH, :]
 
     block = iota2((BLOCKS, HALF), 0)
     spans = [running]
@@ -312,7 +327,7 @@
     out_ref[...] = dot(shared_ref[...], weight_ref[...]).astype(bf16)
 
 
-def call(kernel, count, shapes, scratch=(), space=VMEM, limit=32):
+def call(kernel, count, shapes, scratch=(), space=VMEM, limit=32, cost=None):
     single = len(shapes) == 1
     made = [jax.ShapeDtypeStruct(s, d) for s, d in shapes]
     return pl.pallas_call(
@@ -322,6 +337,7 @@
         out_specs=VMEM if single else [VMEM] * len(shapes),
         scratch_shapes=list(scratch),
         compiler_params=pltpu.CompilerParams(vmem_limit_bytes=limit * 2**20),
+        cost_estimate=cost,
     )
 
 
@@ -355,28 +371,39 @@
         )(tokens, retain)
         stats = lax.all_to_all(own, "span", 0, 0, tiled=True)
     with jax.named_scope("local"):
-        message, scaled, retained, state, pack = call(
-            local_kernel,
-            10,
-            [
-                ((32 * SPANS, WIDTH), bf16),
-                ((LENGTH, WIDTH), f32),
-                ((LENGTH, HALF), f32),
-                ((2 * NDIM * 16, HALF), f32),
-                ((200, WIDTH), f32),
-            ],
-            [pltpu.VMEM((32, WIDTH), f32)],
+        sums, squares, placed, retained, back, pack = call(
+            prepare_kernel,
+            7,
+            [((LENGTH, WIDTH), f32)] * 3 + [((LENGTH, HALF), f32)] * 2 + [((200, WIDTH), f32)],
+            cost=pl.CostEstimate(flops=2 * 10**9, bytes_accessed=2**22, transcendentals=0),
         )(
             tokens,
-            stats,
             retain,
-            norm_gain.reshape(1, WIDTH),
-            norm_bias.reshape(1, WIDTH),
             decay_rate,
             ema_angle,
             ema_input,
             ema_output,
             ema_skip.reshape(1, WIDTH),
+        )
+        message, scaled, state = call(
+            local_kernel,
+            9,
+            [
+                ((32 * SPANS, WIDTH), bf16),
+                ((LENGTH, WIDTH), f32),
+                ((2 * NDIM * 16, HALF), f32),
+            ],
+            [pltpu.VMEM((32, WIDTH), f32)],
+        )(
+            stats,
+            sums,
+            squares,
+            placed,
+            retained,
+            back,
+            pack,
+            norm_gain.reshape(1, WIDTH),
+            norm_bias.reshape(1, WIDTH),
         )
         message = lax.all_to_all(message, "span", 0, 0, tiled=True)
     with jax.named_scope("finish"):

time: 74.3 us -> 74.7 us (level)
  blocking collectives: 61.4 us -> 47 us
  starting transfers between devices: 3.28 us -> 11 us
  waiting for transfers between devices: 1.16 us -> 7.01 us
  local copies, waits for them, and re-layouts: 0.05 us -> 1.35 us
    all_to_all x1 -> x0, blocking collectives: 14.6 us -> none  [shards(): stats = lax.all_to_all(own, 'span', 0, 0, tiled=True)]
    all_to_all x0 -> x1, starting transfers between devices: none -> 7.73 us  [shards(): stats = lax.all_to_all(own, 'span', 0, 0, tiled=True)]
    all_to_all x0 -> x1, waiting for transfers between devices: none -> 5.85 us  [shards(): stats = lax.all_to_all(own, 'span', 0, 0, tiled=True)]
    unnamed x24, local copies, waits for them, and re-layouts: 0.05 us -> 1.35 us
    pallas_call x1 -> x2, Pallas kernels: 1.91 us -> 2.02 us  [the longest x1 1.69 us: shards(): call(local_kernel, 9, [((32 * SPANS, WIDTH), bf16), ((LENGTH, WIDTH), f32...]
  transfers between devices with their start and end apart: 1 -> 2, of which waited for: 1 -> 2; matrix products, arithmetic and copies ran while one was open for 0% -> 0% of each run, Pallas kernels for 0% -> 0%
where the time goes in v3:
time: 74.7 us; the launch traced here: 74.4 us
  blocking collectives  47 us (63%)
  starting transfers between devices  11 us (15%)
  Pallas kernels  7.8 us (10%)
  waiting for transfers between devices  7.01 us (9%)
  local copies, waits for them, and re-layouts  1.35 us (2%)
    all_to_all x1, blocking collectives, shards(): lax.all_to_all(pair, 'tensor', 0, 0, tiled=True, axis_index_groups=groups)  19.1 us
    all_to_all x1, blocking collectives, shards(): lax.all_to_all(copies, 'tensor', 0, 0, tiled=True, axis_index_groups=groups)  12.1 us
    all_to_all x1, blocking collectives, shards(): message = lax.all_to_all(message, 'span', 0, 0, tiled=True)  10.7 us
    all_to_all x1, starting transfers between devices, shards(): stats = lax.all_to_all(own, 'span', 0, 0, tiled=True)  7.73 us
    all_to_all x1, waiting for transfers between devices, shards(): stats = lax.all_to_all(own, 'span', 0, 0, tiled=True)  5.85 us
    all_gather x1, blocking collectives, shards(): lax.all_gather(half, 'tensor', axis=0, tiled=True, axis_index_groups=pairs)  5.1 us
    ppermute x1, starting transfers between devices, shards(): taken = lax.ppermute(give, 'tensor', [(i, i ^ 1) for i in range(16)])  3.28 us
    pallas_call x1, Pallas kernels, shards(): call(finish_kernel, 7, [((HALF, width), bf16), ((HALF, width), bf16)], [p...  2.55 us
  transfers between devices with their start and end apart: 2, of which 2 were waited for; matrix products, arithmetic and copies ran while one was open for 0% of the time, Pallas kernels for 0%

profile of v3, /device:TPU:1, one launch (start us, length us, event | category | flops | bytes accessed | tf_op | source)
XLA Modules:
  0.0 74.4 jit_solution(9747913598535793820)
XLA Ops:
  0.0 2.1 %stats.1 = f32[128,256]{1,0:T(8,128)} custom-call(bf16[256,256]{1,0:T(8,128)(2,1)} %tokens_ref.1, f32[1,256]{1,0:T(1,128)} %bitcast.20), custom_call_target="tpu_custom_call" | custom-call | tf_op jit(solution)/shard_map/stats/pallas_call | solution.py:360
  2.1 0.0 copy-start.2
  2.2 0.0 copy-start.7
  2.2 0.0 copy-start.8
  2.2 0.0 copy-start.10
  2.2 0.0 copy-start.11
  2.2 7.7 %all-to-all-start = ((f32[16,8,256]{2,1,0:T(8,128)}), f32[16,8,256]{2,1,0:T(8,128)S(1)}, u32[]{:S(2)}, u32[]{:S(2)}) async-start(f32[16,8,256]{2,1,0:T(8,128)} %bitcast.27), calls=%async_computation | async-start | bytes 262144 | tf_op jit(solution)/shard_map/stats/all_to_all | solution.py:372
  10.0 0.0 copy-start.4
  10.0 0.6 copy-done.4
  10.6 0.3 local.2
  11.0 5.9 %all-to-all-done = f32[16,8,256]{2,1,0:T(8,128)S(1)} async-done(((f32[16,8,256]{2,1,0:T(8,128)}), f32[16,8,256]{2,1,0:T(8,128)S(1)}, u32[]{:S(2)}, u32[]{:S(2)}) %all-to-all-start) | async-done | bytes 131104 | tf_op jit(solution)/shard_map/stats/all_to_all | solution.py:372
  16.8 0.7 copy-done.5
  17.5 1.7 %local.3 = (bf16[512,256]{1,0:T(8,128)(2,1)S(1)}, f32[256,256]{1,0:T(8,128)S(1)}, f32[512,128]{1,0:T(8,128)S(1)}) custom-call(f32[128,256]{1,0:T(8,128)S(1)} %bitcast.13, f32[256,256]{1,0:T(8,128)S(1)} %get-tuple-element.16.sums_ref, f32[256,256]{1,0:T(8,128)S(1)} %get-tuple-element.17.squares_ref, f32[256,256]{1,0:T(8,128)S(1)} %get-tuple-element.18.placed_ref, ...), custom_call_target="tpu_custom_call" | custom-call | tf_op jit(solution)/shard_map/local/pallas_call | solution.py:388
  19.2 10.7 %all_to_all.45 = bf16[16,32,256]{2,1,0:T(8,128)(2,1)S(1)} all-to-all(bf16[16,32,256]{2,1,0:T(8,128)(2,1)S(1)} %bitcast.18), channel_id=1, replica_groups=mesh['span'=16,'tensor'=16] {'span'}, dimensions={0} | all-to-all | bytes 524288 | tf_op jit(solution)/shard_map/local/all_to_all | solution.py:408
  30.0 2.6 %finish.1 = (bf16[128,1024]{1,0:T(8,128)(2,1)S(1)}, bf16[128,1024]{1,0:T(8,128)(2,1)S(1)}) custom-call(bf16[512,256]{1,0:T(8,128)(2,1)S(1)} %bitcast.15, f32[128,256]{1,0:T(8,128)S(1)} %bitcast.14, f32[256,256]{1,0:T(8,128)S(1)} %get-tuple-element.23.scaled_ref, f32[256,128]{1,0:T(8,128)S(1)} %get-tuple-element.19.retained_ref, ...), custom_call_target="tpu_custom_call" | custom-call | tf_op jit(solution)/shard_map/finish/pallas_call | solution.py:411
  32.5 3.3 %collective-permute-start = (bf16[128,1024]{1,0:T(8,128)(2,1)S(1)}, bf16[128,1024]{1,0:T(8,128)(2,1)S(1)}, u32[]{:S(2)}, u32[]{:S(2)}) collective-permute-start(bf16[128,1024]{1,0:T(8,128)(2,1)S(1)} %get-tuple-element.25), channel_id=1, source_target_pairs={{0,1},{1,0},{2,3},{3,2},{4,5},{5,4},{6,7},{7,6},{8,9},{9,8},{10,11... | collective-permute-start | bytes 786440 | tf_op jit(solution)/shard_map/shared/ppermute | solution.py:426
  35.8 1.2 %collective-permute-done = bf16[128,1024]{1,0:T(8,128)(2,1)S(1)} collective-permute-done((bf16[128,1024]{1,0:T(8,128)(2,1)S(1)}, bf16[128,1024]{1,0:T(8,128)(2,1)S(1)}, u32[]{:S(2)}, u32[]{:S(2)}) %collective-permute-start) | collective-permute-done | bytes 262176 | tf_op jit(solution)/shard_map/shared/ppermute | solution.py:426
  37.0 0.1 add_convert_fusion
  37.0 0.0 copy-start.3
  37.0 19.1 %all_to_all.46 = bf16[8,16,1024]{2,1,0:T(8,128)(2,1)S(1)} all-to-all(bf16[8,16,1024]{2,1,0:T(8,128)(2,1)S(1)} %bitcast.25), channel_id=1, replica_groups={{0,2,4,6,8,10,12,14},{1,3,5,7,9,11,13,15},{16,18,20,22,24,26,28,30},{17..., dimensions={0} | all-to-all | bytes 524288 | tf_op jit(solution)/shard_map/shared/all_to_all | solution.py:429
  56.1 0.1 shared.1
  56.3 12.1 %all_to_all.47 = bf16[8,16,1024]{2,1,0:T(8,128)(2,1)S(1)} all-to-all(bf16[8,16,1024]{2,1,0:T(8,128)(2,1)S(1)} %bitcast.17), channel_id=1, replica_groups={{0,2,4,6,8,10,12,14},{1,3,5,7,9,11,13,15},{16,18,20,22,24,26,28,30},{17..., dimensions={0} | all-to-all | bytes 524288 | tf_op jit(solution)/shard_map/output/all_to_all | solution.py:432
  68.3 5.1 %all_gather.3.shared_ref = bf16[256,1024]{1,0:T(8,128)(2,1)S(1)} all-gather(bf16[128,1024]{1,0:T(8,128)(2,1)S(1)} %bitcast.26), channel_id=1, replica_groups={{0,1},{2,3},{4,5},{6,7},{8,9},{10,11},{12,13},{14,15},{16,17},{18,19},{..., dimensions={0}, use_global_device_ids=true | all-gather | bytes 786432 | tf_op jit(solution)/shard_map/output/all_gather | solution.py:434
  73.4 1.0 %output.1 = bf16[256,256]{1,0:T(8,128)(2,1)} custom-call(bf16[256,1024]{1,0:T(8,128)(2,1)S(1)} %all_gather.3.shared_ref, bf16[1024,256]{1,0:T(8,128)(2,1)S(1)} %copy-done.1), custom_call_target="tpu_custom_call" | custom-call | tf_op jit(solution)/shard_map/output/pallas_call | solution.py:435
  (15 shorter events, 0.0 us)
Async XLA Ops:
  2.1 7.8 %copy-start.2 = (bf16[256,256]{1,0:T(8,128)(2,1)S(1)}, bf16[256,256]{1,0:T(8,128)(2,1)}, u32[]{:S(2)}) copy-start(bf16[256,256]{1,0:T(8,128)(2,1)} %tokens_ref.1) | copy-start | bytes 393220
  2.2 7.8 %copy-start.7 = (f32[2,16,256]{2,1,0:T(8,128)S(1)}, f32[2,16,256]{2,1,0:T(8,128)}, u32[]{:S(2)}) copy-start(f32[2,16,256]{2,1,0:T(8,128)} %output_ref.1) | copy-start | bytes 98308
  2.2 7.8 %copy-start.8 = (f32[16,256]{1,0:T(8,128)S(1)}, f32[16,256]{1,0:T(8,128)}, u32[]{:S(2)}) copy-start(f32[16,256]{1,0:T(8,128)} %decay_ref.1) | copy-start | bytes 49156
  2.2 7.8 %copy-start.9 = (f32[16,256]{1,0:T(8,128)S(1)}, f32[16,256]{1,0:T(8,128)}, u32[]{:S(2)}) copy-start(f32[16,256]{1,0:T(8,128)} %angle_ref.1) | copy-start | bytes 49156
  2.2 7.8 %copy-start.10 = (f32[16,256]{1,0:T(8,128)S(1)}, f32[16,256]{1,0:T(8,128)}, u32[]{:S(2)}) copy-start(f32[16,256]{1,0:T(8,128)} %input_ref.1) | copy-start | bytes 49156
  2.2 7.8 %copy-start.11 = (f32[256]{0:T(256)S(1)}, f32[256]{0:T(256)}, u32[]{:S(2)}) copy-start(f32[256]{0:T(256)} %param.20) | copy-start | bytes 3076
  2.2 14.6 %all-to-all-start = ((f32[16,8,256]{2,1,0:T(8,128)}), f32[16,8,256]{2,1,0:T(8,128)S(1)}, u32[]{:S(2)}, u32[]{:S(2)}) async-start(f32[16,8,256]{2,1,0:T(8,128)} %bitcast.27), calls=%async_computation | async-start | bytes 262144 | tf_op jit(solution)/shard_map/stats/all_to_all | solution.py:372
  10.0 0.7 copy-start.4
  10.6 6.2 %copy-start.6 = (f32[256]{0:T(256)S(1)}, f32[256]{0:T(256)}, u32[]{:S(2)}) copy-start(f32[256]{0:T(256)} %param.15) | copy-start | bytes 3076
  16.8 0.7 copy-start.5
  19.2 10.8 %copy-start = (bf16[256,1024]{1,0:T(8,128)(2,1)S(1)}, bf16[256,1024]{1,0:T(8,128)(2,1)}, u32[]{:S(2)}) copy-start(bf16[256,1024]{1,0:T(8,128)(2,1)} %weight_ref.2) | copy-start | bytes 1572868
  32.5 4.4 %collective-permute-start = (bf16[128,1024]{1,0:T(8,128)(2,1)S(1)}, bf16[128,1024]{1,0:T(8,128)(2,1)S(1)}, u32[]{:S(2)}, u32[]{:S(2)}) collective-permute-start(bf16[128,1024]{1,0:T(8,128)(2,1)S(1)} %get-tuple-element.25), channel_id=1, source_target_pairs={{0,1},{1,0},{2,3},{3,2},{4,5},{5,4},{6,7},{7,6},{8,9},{9,8},{10,11... | collective-permute-start | bytes 786440 | tf_op jit(solution)/shard_map/shared/ppermute | solution.py:426
  37.0 19.1 %copy-start.3 = (f32[1024]{0:T(1024)S(1)}, f32[1024]{0:T(1024)}, u32[]{:S(2)}) copy-start(f32[1024]{0:T(1024)} %param.22) | copy-start | bytes 12292
  68.3 5.1 %copy-start.1 = (bf16[1024,256]{1,0:T(8,128)(2,1)S(1)}, bf16[1024,256]{1,0:T(8,128)(2,1)}, u32[]{:S(2)}) copy-start(bf16[1024,256]{1,0:T(8,128)(2,1)} %weight_ref.3) | copy-start | bytes 1572868

commit v4 on v3

--- a/solution.py
+++ b/solution.py
@@ -53,15 +53,7 @@
     return ar * br - ai * bi, ar * bi + ai * br
 
 
-def stats_kernel(tokens_hbm, retain_hbm, out_ref, tokens_ref, retain_ref, arrived):
-    copies = (
-        pltpu.make_async_copy(tokens_hbm, tokens_ref, arrived.at[0]),
-        pltpu.make_async_copy(retain_hbm, retain_ref, arrived.at[1]),
-    )
-    for copy in copies:
-        copy.start()
-    for copy in copies:
-        copy.wait()
+def stats_kernel(tokens_ref, retain_ref, out_ref):
     values = tokens_ref[...].astype(f32)
     total = jnp.sum(values, axis=0, keepdims=True)
     squares = jnp.sum(values * values, axis=0, keepdims=True)
@@ -84,12 +76,17 @@
     input_ref,
     output_ref,
     skip_ref,
+    gain_ref,
+    bias_ref,
     sums_ref,
     squares_ref,
     placed_ref,
     retained_ref,
     back_ref,
     pack_ref,
+    leave_ref,
+    enter_ref,
+    power_ref,
 ):
     tokens = tokens_ref[...]
     row = time_of(iota2((LENGTH, LENGTH), 0))
@@ -121,6 +118,8 @@
     pack_ref[32:48, :] = output_ref[0] * weight
     pack_ref[48:64, :] = output_ref[1] * weight
     pack_ref[192:200, :] = jnp.broadcast_to(skip_ref[...], (8, WIDTH))
+    pack_ref[200:208, :] = jnp.broadcast_to(gain_ref[...], (8, WIDTH))
+    pack_ref[208:216, :] = jnp.broadcast_to(bias_ref[...], (8, WIDTH))
     at_re, at_im = power_re, power_im
     for k in range(1, 9):
         at_re, at_im = cmul(at_re, at_im, at_re, at_im)
@@ -129,19 +128,51 @@
             pack_ref[place : place + 16, :] = at_re
             pack_ref[place + 16 : place + 32, :] = at_im
 
+    block = iota2((BLOCKS, HALF), 0)
+    after = running
+    ahead = jnp.where(block >= 1, pltpu.roll(running, 1, 0), 1.0)
+    for k in range(3):
+        after = after * jnp.where(block < BLOCKS - 2**k, pltpu.roll(after, BLOCKS - 2**k, 0), 1.0)
+        ahead = ahead * jnp.where(block >= 2**k, pltpu.roll(ahead, 2**k, 0), 1.0)
+
+    at_re, at_im = jnp.ones_like(power_re), jnp.zeros_like(power_re)
+    for step in range(STEPS):
+        power_ref[32 * step : 32 * step + 16, :] = at_re
+        power_ref[32 * step + 16 : 32 * step + 32, :] = at_im
+        at_re, at_im = cmul(at_re, at_im, power_re, power_im)
+
+    def wide(place):
+        return jnp.broadcast_to(pack_ref[place : place + 1, lanes], (BLOCKS, HALF))
+
+    for h in range(2):
+        lanes = slice(HALF * h, HALF * h + HALF)
+        for j in range(NDIM):
+            out_re, out_im = after, jnp.zeros_like(after)
+            in_re, in_im = cmul(ahead * wide(32 + j), ahead * wide(48 + j), wide(j), wide(16 + j))
+            for k in range(3):
+                far_re, far_im = wide(64 + 32 * k + j), wide(80 + 32 * k + j)
+                chosen = (block // 2**k) % 2 == 1
+                on_re, on_im = cmul(in_re, in_im, far_re, far_im)
+                in_re, in_im = jnp.where(chosen, on_re, in_re), jnp.where(chosen, on_im, in_im)
+                on_re, on_im = cmul(out_re, out_im, far_re, far_im)
+                out_re, out_im = jnp.where(chosen, out_re, on_re), jnp.where(chosen, out_im, on_im)
+            leave_ref[16 * j : 16 * j + 8, lanes] = out_re
+            leave_ref[16 * j + 8 : 16 * j + 16, lanes] = out_im
+            enter_ref[16 * j : 16 * j + 8, lanes] = in_re
+            enter_ref[16 * j + 8 : 16 * j + 16, lanes] = in_im
+
+
 def local_kernel(
     stats_ref,
     sums_ref,
     squares_ref,
     placed_ref,
-    retained_ref,
     back_ref,
     pack_ref,
-    gain_ref,
-    bias_ref,
+    leave_ref,
+    power_ref,
     message_ref,
     scaled_ref,
-    state_ref,
     summary,
 ):
     me = lax.axis_index("span")
@@ -157,12 +188,40 @@
     average = cum_sum * share
     spread = cum_sq * share - average * average
     inverse = lax.rsqrt(spread + norm_eps)
-    normed = (placed_ref[...] - average) * inverse * gain_ref[...] + bias_ref[...]
+    normed = (placed_ref[...] - average) * inverse * pack_ref[200:201, :] + pack_ref[208:209, :]
     back = back_ref[...]
     scaled_ref[...] = normed * jnp.concatenate([back, back], axis=1)
+
+    for h in range(2):
+        lanes = slice(HALF * h, HALF * h + HALF)
+        for first in range(0, NDIM, CHUNK):
+
+            u = scaled_ref[LENGTH - BLOCKS : LENGTH, lanes]
+            ends = [u] * CHUNK + [u * 0.0] * CHUNK
+            for step in range(1, STEPS):
+                row = LENGTH - BLOCKS * (step + 1)
+                u = scaled_ref[row : row + BLOCKS, lanes]
+                for n in range(2 * CHUNK):
+                    place = 32 * step + 16 * (n // CHUNK) + first + n % CHUNK
+                    ends[n] = ends[n] + u * power_ref[place : place + 1, lanes]
+            for n in range(CHUNK):
+                j = first + n
+                end_re, end_im = cmul(
+                    ends[n],
+                    ends[CHUNK + n],
+                    leave_ref[16 * j : 16 * j + 8, lanes],
+                    leave_ref[16 * j + 8 : 16 * j + 16, lanes],
+                )
+                summary[j : j + 1, lanes] = jnp.sum(end_re, axis=0, keepdims=True)
+                summary[16 + j : 17 + j, lanes] = jnp.sum(end_im, axis=0, keepdims=True)
+    sent = summary[...].astype(bf16)
+    for i in range(SPANS):
+        message_ref[32 * i : 32 * i + 32, :] = sent
+
+
+def within_kernel(scaled_ref, retained_ref, pack_ref, mixed):
+    block = iota2((BLOCKS, HALF), 0)
     running = retained_ref[LENGTH - BLOCKS : LENGTH, :]
-
-    block = iota2((BLOCKS, HALF), 0)
     spans = [running]
     for k in range(2):
         reach = spans[-1]
@@ -180,7 +239,7 @@
             re_of = [wide(j, lanes) for j in js]
             im_of = [wide(16 + j, lanes) for j in js]
 
-            def step_on(step, held):
+            def end_on(step, held):
                 u = scaled_ref[pl.ds(pl.multiple_of(step * BLOCKS, BLOCKS), BLOCKS), lanes]
                 following = []
                 for n in range(CHUNK):
@@ -194,7 +253,8 @@
             begin = []
             for n in range(CHUNK):
                 begin += [u0 * re_of[n] + u1, u0 * im_of[n]]
-            ends = lax.fori_loop(2, STEPS, step_on, tuple(begin), unroll=3)
+            ends = lax.fori_loop(2, STEPS, end_on, tuple(begin), unroll=3)
+            begin = []
             for n, j in enumerate(js):
                 re, im = running * ends[2 * n], running * ends[2 * n + 1]
                 for k in range(3):
@@ -205,79 +265,10 @@
                         wide(80 + 32 * k + j, lanes),
                     )
                     re, im = re + spans[k] * add_re, im + spans[k] * add_im
-                summary[j : j + 1, lanes] = re[7:8]
-                summary[16 + j : 17 + j, lanes] = im[7:8]
-                place = (h * NDIM + j) * 16
-                state_ref[place : place + 8, :] = jnp.where(block >= 1, pltpu.roll(re, 1, 0), 0.0)
-                state_ref[place + 8 : place + 16, :] = jnp.where(
-                    block >= 1, pltpu.roll(im, 1, 0), 0.0
-                )
-    sent = summary[...].astype(bf16)
-    for i in range(SPANS):
-        message_ref[32 * i : 32 * i + 32, :] = sent
-
-
-def finish_kernel(
-    message_ref,
-    stats_ref,
-    scaled_ref,
-    retained_ref,
-    state_ref,
-    pack_ref,
-    weight_ref,
-    give_ref,
-    keep_ref,
-    entering,
-    mixed,
-):
-    me = lax.axis_index("span")
-    core = lax.axis_index("tensor") % 2
-    far_re, far_im = pack_ref[160:176, :], pack_ref[176:192, :]
-
-    def turn(i, held):
-        kept = stats_ref[pl.ds(i * 8 + 2, 1), :]
-        piece = message_ref[pl.ds(pl.multiple_of(i * 32, 32), 32), :].astype(f32)
-        re, im = cmul(held[0], held[1], far_re, far_im)
-        return re * kept + piece[:16], im * kept + piece[16:]
-
-    start = jnp.zeros((NDIM, WIDTH), f32)
-    state_re, state_im = lax.fori_loop(0, me, turn, (start, start))
-    entering[0:16, :] = state_re
-    entering[16:32, :] = state_im
-
-    block = iota2((BLOCKS, HALF), 0)
-    closing = retained_ref[LENGTH - BLOCKS : LENGTH, :]
-    ahead = jnp.where(block >= 1, pltpu.roll(closing, 1, 0), 1.0)
-    for k in range(3):
-        ahead = ahead * jnp.where(block >= 2**k, pltpu.roll(ahead, 2**k, 0), 1.0)
-
-    def wide(ref, place, lanes):
-        return jnp.broadcast_to(ref[place : place + 1, lanes], (BLOCKS, HALF))
-
-    for h in range(2):
-        lanes = slice(HALF * h, HALF * h + HALF)
-        for first in range(0, NDIM, CHUNK):
-            js = range(first, first + CHUNK)
-            begin = []
-            for j in js:
-                re = ahead * wide(entering, j, lanes)
-                im = ahead * wide(entering, 16 + j, lanes)
-                for k in range(3):
-                    on_re, on_im = cmul(
-                        re,
-                        im,
-                        wide(pack_ref, 64 + 32 * k + j, lanes),
-                        wide(pack_ref, 80 + 32 * k + j, lanes),
-                    )
-                    chosen = (block // 2**k) % 2 == 1
-                    re, im = jnp.where(chosen, on_re, re), jnp.where(chosen, on_im, im)
-                place = (h * NDIM + j) * 16
-                begin.append(re + state_ref[place : place + 8, :])
-                begin.append(im + state_ref[place + 8 : place + 16, :])
-            re_of = [wide(pack_ref, j, lanes) for j in js]
-            im_of = [wide(pack_ref, 16 + j, lanes) for j in js]
-            out_re = [wide(pack_ref, 32 + j, lanes) for j in js]
-            out_im = [wide(pack_ref, 48 + j, lanes) for j in js]
+                begin.append(jnp.where(block >= 1, pltpu.roll(re, 1, 0), 0.0))
+                begin.append(jnp.where(block >= 1, pltpu.roll(im, 1, 0), 0.0))
+            out_re = [wide(32 + j, lanes) for j in js]
+            out_im = [wide(48 + j, lanes) for j in js]
             skip = pack_ref[192:200, lanes]
 
             def step_on(step, held):
@@ -301,6 +292,61 @@
 
             lax.fori_loop(0, STEPS, step_on, tuple(begin), unroll=2)
 
+
+def finish_kernel(
+    message_ref,
+    stats_ref,
+    mixed_ref,
+    retained_ref,
+    pack_ref,
+    enter_ref,
+    power_ref,
+    weight_ref,
+    give_ref,
+    keep_ref,
+    entering,
+    mixed,
+):
+    me = lax.axis_index("span")
+    core = lax.axis_index("tensor") % 2
+    far_re, far_im = pack_ref[160:176, :], pack_ref[176:192, :]
+
+    def turn(i, held):
+        kept = stats_ref[pl.ds(i * 8 + 2, 1), :]
+        piece = message_ref[pl.ds(pl.multiple_of(i * 32, 32), 32), :].astype(f32)
+        re, im = cmul(held[0], held[1], far_re, far_im)
+        return re * kept + piece[:16], im * kept + piece[16:]
+
+    start = jnp.zeros((NDIM, WIDTH), f32)
+    state_re, state_im = lax.fori_loop(0, me, turn, (start, start))
+    entering[0:16, :] = state_re
+    entering[16:32, :] = state_im
+
+    for h in range(2):
+        lanes = slice(HALF * h, HALF * h + HALF)
+        for first in range(0, NDIM, CHUNK):
+            held = []
+            for j in range(first, first + CHUNK):
+                held.append(
+                    cmul(
+                        jnp.broadcast_to(entering[j : j + 1, lanes], (BLOCKS, HALF)),
+                        jnp.broadcast_to(entering[16 + j : 17 + j, lanes], (BLOCKS, HALF)),
+                        enter_ref[16 * j : 16 * j + 8, lanes],
+                        enter_ref[16 * j + 8 : 16 * j + 16, lanes],
+                    )
+                )
+            for step in range(STEPS):
+                rows = slice(BLOCKS * step, BLOCKS * step + BLOCKS)
+                terms = [
+                    re * power_ref[32 * step + first + n : 32 * step + first + n + 1, lanes]
+                    - im * power_ref[32 * step + 16 + first + n : 32 * step + 17 + first + n, lanes]
+                    for n, (re, im) in enumerate(held)
+                ]
+                while len(terms) > 1:
+                    terms = [terms[i] + terms[i + 1] for i in range(0, len(terms), 2)]
+                so_far = mixed_ref[rows, lanes] if first == 0 else mixed[rows, lanes]
+                mixed[rows, lanes] = so_far + terms[0]
+
     retained = retained_ref[...]
     ema = jnp.concatenate([retained, retained], axis=1) * mixed[...]
     active = (ema / (1.0 + jnp.exp(-ema))).astype(bf16)
@@ -323,8 +369,15 @@
         out_ref[16 * i : 16 * i + 16, :] = normed
 
 
-def output_kernel(shared_ref, weight_ref, out_ref):
+def own_kernel(shared_ref, weight_ref, out_ref):
     out_ref[...] = dot(shared_ref[...], weight_ref[...]).astype(bf16)
+
+
+def other_kernel(shared_ref, weight_ref, own_ref, out_ref):
+    core = lax.axis_index("tensor") % 2
+    other = dot(shared_ref[...], weight_ref[...]).astype(bf16)
+    out_ref[pl.ds(pl.multiple_of(core * HALF, HALF), HALF), :] = own_ref[...]
+    out_ref[pl.ds(pl.multiple_of((1 - core) * HALF, HALF), HALF), :] = other
 
 
 def call(kernel, count, shapes, scratch=(), space=VMEM, limit=32, cost=None):
@@ -361,20 +414,19 @@
             stats_kernel,
             2,
             [((8 * SPANS, WIDTH), f32)],
-            [
-                pltpu.VMEM((LENGTH, WIDTH), bf16),
-                pltpu.VMEM((1, LENGTH), f32),
-                pltpu.SemaphoreType.DMA((2,)),
-            ],
-            pl.BlockSpec(memory_space=pltpu.HBM),
-            60,
+            limit=16,
         )(tokens, retain)
         stats = lax.all_to_all(own, "span", 0, 0, tiled=True)
     with jax.named_scope("local"):
-        sums, squares, placed, retained, back, pack = call(
+        sums, squares, placed, retained, back, pack, leave, enter, power = call(
             prepare_kernel,
-            7,
-            [((LENGTH, WIDTH), f32)] * 3 + [((LENGTH, HALF), f32)] * 2 + [((200, WIDTH), f32)],
+            9,
+            [((LENGTH, WIDTH), f32)] * 3
+            + [((LENGTH, HALF), f32)] * 2
+            + [((216, WIDTH), f32)]
+            + [((2 * NDIM * BLOCKS, WIDTH), f32)] * 2
+            + [((2 * NDIM * STEPS, WIDTH), f32)],
+            limit=16,
             cost=pl.CostEstimate(flops=2 * 10**9, bytes_accessed=2**22, transcendentals=0),
         )(
             tokens,
@@ -384,55 +436,53 @@
             ema_input,
             ema_output,
             ema_skip.reshape(1, WIDTH),
-        )
-        message, scaled, state = call(
-            local_kernel,
-            9,
-            [
-                ((32 * SPANS, WIDTH), bf16),
-                ((LENGTH, WIDTH), f32),
-                ((2 * NDIM * 16, HALF), f32),
-            ],
-            [pltpu.VMEM((32, WIDTH), f32)],
-        )(
-            stats,
-            sums,
-            squares,
-            placed,
-            retained,
-            back,
-            pack,
             norm_gain.reshape(1, WIDTH),
             norm_bias.reshape(1, WIDTH),
         )
+        message, scaled = call(
+            local_kernel,
+            8,
+            [((32 * SPANS, WIDTH), bf16), ((LENGTH, WIDTH), f32)],
+            [pltpu.VMEM((32, WIDTH), f32)],
+            limit=16,
+        )(stats, sums, squares, placed, back, pack, leave, power)
         message = lax.all_to_all(message, "span", 0, 0, tiled=True)
+        mixed = call(
+            within_kernel,
+            3,
+            [((LENGTH, WIDTH), f32)],
+            limit=16,
+            cost=pl.CostEstimate(flops=2 * 10**9, bytes_accessed=2**22, transcendentals=0),
+        )(scaled, retained, pack)
     with jax.named_scope("finish"):
         width = shared_weight.shape[1]
         give, keep = call(
             finish_kernel,
-            7,
+            8,
             [((HALF, width), bf16), ((HALF, width), bf16)],
             [pltpu.VMEM((32, WIDTH), f32), pltpu.VMEM((LENGTH, WIDTH), f32)],
-        )(
-            message,
-            stats,
-            scaled,
-            retained,
-            state,
-            pack,
-            shared_weight,
-        )
+            limit=16,
+        )(message, stats, mixed, retained, pack, enter, power, shared_weight)
     with jax.named_scope("shared"):
-        taken = lax.ppermute(give, "tensor", [(i, i ^ 1) for i in range(16)])
+        swap = [(i, i ^ 1) for i in range(16)]
+        taken = lax.ppermute(give, "tensor", swap)
         pair = (taken.astype(f32) + keep.astype(f32)).astype(bf16)
         groups = [[core + 2 * z for z in range(8)] for core in range(2)]
         parts = lax.all_to_all(pair, "tensor", 0, 0, tiled=True, axis_index_groups=groups)
         copies = call(norm_kernel, 2, [((HALF, width), bf16)])(parts, shared_gain.reshape(1, width))
     with jax.named_scope("output"):
         half = lax.all_to_all(copies, "tensor", 0, 0, tiled=True, axis_index_groups=groups)
-        pairs = [[2 * z, 2 * z + 1] for z in range(8)]
-        whole = lax.all_gather(half, "tensor", axis=0, tiled=True, axis_index_groups=pairs)
-        return call(output_kernel, 2, [((LENGTH, WIDTH), bf16)])(whole, output_weight)
+        other = lax.ppermute(half, "tensor", swap)
+        own = call(
+            own_kernel,
+            2,
+            [((HALF, WIDTH), bf16)],
+            limit=16,
+            cost=pl.CostEstimate(flops=10**9, bytes_accessed=2**20, transcendentals=0),
+        )(half, output_weight)
+        return call(other_kernel, 3, [((LENGTH, WIDTH), bf16)], limit=16)(
+            other, output_weight, own
+        )
 
 
 def solution(mesh):

time: 74.7 us -> 72.9 us (0.976)
  blocking collectives: 47 us -> 31.3 us
  starting transfers between devices: 11 us -> 17.7 us
  waiting for transfers between devices: 7.01 us -> 11.7 us
  Pallas kernels: 7.8 us -> 9.39 us
  local copies, waits for them, and re-layouts: 1.35 us -> 2.24 us
    all_to_all x1 -> x0, blocking collectives: 10.7 us -> none  [shards(): message = lax.all_to_all(message, 'span', 0, 0, tiled=True)]
    all_gather x1 -> x0, blocking collectives: 5.1 us -> none  [shards(): lax.all_gather(half, 'tensor', axis=0, tiled=True, axis_index_groups=pairs)]
    all_to_all x0 -> x1, waiting for transfers between devices: none -> 4.08 us  [shards(): message = lax.all_to_all(message, 'span', 0, 0, tiled=True)]
    all_to_all x0 -> x1, starting transfers between devices: none -> 3.53 us  [shards(): message = lax.all_to_all(message, 'span', 0, 0, tiled=True)]
    ppermute x1 -> x2, starting transfers between devices: 3.28 us -> 6.4 us  [the longest x1 3.23 us: shards(): taken = lax.ppermute(give, 'tensor', swap)]
    pallas_call x5 -> x7, Pallas kernels: 7.67 us -> 9.26 us  [the longest x1 3.23 us: shards(): call(within_kernel, 3, [((LENGTH, WIDTH), f32)], limit=16, cost=pl.CostEs...]
    ppermute x1 -> x2, waiting for transfers between devices: 1.16 us -> 2.08 us  [the longest x1 1.16 us: shards(): taken = lax.ppermute(give, 'tensor', swap)]
    unnamed x24 -> x26, local copies, waits for them, and re-layouts: 1.35 us -> 2.24 us
  transfers between devices with their start and end apart: 2 -> 4, of which waited for: 2 -> 4; matrix products, arithmetic and copies ran while one was open for 0% -> 0% of each run, Pallas kernels for 0% -> 6%
where the time goes in v4:
time: 72.9 us; the launch traced here: 72.5 us
  blocking collectives  31.3 us (43%)
  starting transfers between devices  17.7 us (24%)
  waiting for transfers between devices  11.7 us (16%)
  Pallas kernels  9.39 us (13%)
  local copies, waits for them, and re-layouts  2.24 us (3%)
    all_to_all x1, blocking collectives, shards(): lax.all_to_all(pair, 'tensor', 0, 0, tiled=True, axis_index_groups=groups)  19.1 us
    all_to_all x1, blocking collectives, shards(): lax.all_to_all(copies, 'tensor', 0, 0, tiled=True, axis_index_groups=groups)  12.2 us
    all_to_all x1, starting transfers between devices, shards(): stats = lax.all_to_all(own, 'span', 0, 0, tiled=True)  7.73 us
    all_to_all x1, waiting for transfers between devices, shards(): stats = lax.all_to_all(own, 'span', 0, 0, tiled=True)  5.55 us
    all_to_all x1, waiting for transfers between devices, shards(): message = lax.all_to_all(message, 'span', 0, 0, tiled=True)  4.08 us
    all_to_all x1, starting transfers between devices, shards(): message = lax.all_to_all(message, 'span', 0, 0, tiled=True)  3.53 us
    pallas_call x1, Pallas kernels, shards(): call(within_kernel, 3, [((LENGTH, WIDTH), f32)], limit=16, cost=pl.CostEs...  3.23 us
    ppermute x1, starting transfers between devices, shards(): taken = lax.ppermute(give, 'tensor', swap)  3.23 us
  transfers between devices with their start and end apart: 4, of which 4 were waited for; matrix products, arithmetic and copies ran while one was open for 0% of the time, Pallas kernels for 6%

profile of v4, /device:TPU:1, one launch (start us, length us, event | category | flops | bytes accessed | tf_op | source)
XLA Modules:
  0.0 72.5 jit_solution(39402726058723062)
XLA Ops:
  0.0 0.7 copy-done.5
  0.7 0.9 %copy-done.2 = bf16[256,256]{1,0:T(8,128)(2,1)S(1)} copy-done((bf16[256,256]{1,0:T(8,128)(2,1)S(1)}, bf16[256,256]{1,0:T(8,128)(2,1)}, u32[]{:S(2)}) %copy-start.2) | copy-done | bytes 131096
  1.6 1.2 %stats.1 = f32[128,256]{1,0:T(8,128)} custom-call(bf16[256,256]{1,0:T(8,128)(2,1)S(1)} %copy-done.2, f32[1,256]{1,0:T(1,128)S(1)} %bitcast.21), custom_call_target="tpu_custom_call" | custom-call | tf_op jit(solution)/shard_map/stats/pallas_call | solution.py:413
  2.8 0.0 copy-start.12
  2.8 7.7 %all-to-all-start = ((f32[16,8,256]{2,1,0:T(8,128)}), f32[16,8,256]{2,1,0:T(8,128)S(1)}, u32[]{:S(2)}, u32[]{:S(2)}) async-start(f32[16,8,256]{2,1,0:T(8,128)} %bitcast.1), calls=%async_computation | async-start | bytes 262144 | tf_op jit(solution)/shard_map/stats/all_to_all | solution.py:419
  10.7 0.6 copy-done.10
  11.3 0.6 local.3
  11.9 5.5 %all-to-all-done = f32[16,8,256]{2,1,0:T(8,128)S(1)} async-done(((f32[16,8,256]{2,1,0:T(8,128)}), f32[16,8,256]{2,1,0:T(8,128)S(1)}, u32[]{:S(2)}, u32[]{:S(2)}) %all-to-all-start) | async-done | bytes 131104 | tf_op jit(solution)/shard_map/stats/all_to_all | solution.py:419
  17.4 2.0 %local.4 = (bf16[512,256]{1,0:T(8,128)(2,1)}, f32[256,256]{1,0:T(8,128)S(1)}) custom-call(f32[128,256]{1,0:T(8,128)S(1)} %bitcast.13, f32[256,256]{1,0:T(8,128)S(1)} %get-tuple-element.18.sums_ref, f32[256,256]{1,0:T(8,128)S(1)} %get-tuple-element.19.squares_ref, f32[256,256]{1,0:T(8,128)S(1)} %get-tuple-element.20.placed_ref, ...), custom_call_target="tpu_custom_call" | custom-call | tf_op jit(solution)/shard_map/local/pallas_call | solution.py:442
  19.4 3.5 %all-to-all-start.1 = ((bf16[16,32,256]{2,1,0:T(8,128)(2,1)}), bf16[16,32,256]{2,1,0:T(8,128)(2,1)S(1)}, u32[]{:S(2)}, u32[]{:S(2)}) async-start(bf16[16,32,256]{2,1,0:T(8,128)(2,1)} %bitcast.6), calls=%async_computation.1 | async-start | bytes 524288 | tf_op jit(solution)/shard_map/local/all_to_all | solution.py:449
  23.0 3.2 %local.5.mixed_ref = f32[256,256]{1,0:T(8,128)S(1)} custom-call(f32[256,256]{1,0:T(8,128)S(1)} %get-tuple-element.26.scaled_ref, f32[256,128]{1,0:T(8,128)S(1)} %get-tuple-element.27.retained_ref, f32[216,256]{1,0:T(8,128)S(1)} %get-tuple-element.22.pack_ref), custom_call_target="tpu_custom_call" | custom-call | flops 2000000000 | bytes 4194304 | tf_op jit(solution)/shard_map/local/pallas_call | solution.py:450
  26.2 4.1 %all-to-all-done.1 = bf16[16,32,256]{2,1,0:T(8,128)(2,1)S(1)} async-done(((bf16[16,32,256]{2,1,0:T(8,128)(2,1)}), bf16[16,32,256]{2,1,0:T(8,128)(2,1)S(1)}, u32[]{:S(2)}, u32[]{:S(2)}) %all-to-all-start.1) | async-done | bytes 262176 | tf_op jit(solution)/shard_map/local/all_to_all | solution.py:449
  30.3 1.1 %finish.1 = (bf16[128,1024]{1,0:T(8,128)(2,1)S(1)}, bf16[128,1024]{1,0:T(8,128)(2,1)S(1)}) custom-call(bf16[512,256]{1,0:T(8,128)(2,1)S(1)} %bitcast.17, f32[128,256]{1,0:T(8,128)S(1)} %bitcast.14, f32[256,256]{1,0:T(8,128)S(1)} %local.5.mixed_ref, f32[256,128]{1,0:T(8,128)S(1)} %get-tuple-element.27.retained_ref, ...), custom_call_target="tpu_custom_call" | custom-call | tf_op jit(solution)/shard_map/finish/pallas_call | solution.py:459
  31.4 3.2 %collective-permute-start = (bf16[128,1024]{1,0:T(8,128)(2,1)S(1)}, bf16[128,1024]{1,0:T(8,128)(2,1)S(1)}, u32[]{:S(2)}, u32[]{:S(2)}) collective-permute-start(bf16[128,1024]{1,0:T(8,128)(2,1)S(1)} %get-tuple-element.29), channel_id=1, source_target_pairs={{0,1},{1,0},{2,3},{3,2},{4,5},{5,4},{6,7},{7,6},{8,9},{9,8},{10,11... | collective-permute-start | bytes 786440 | tf_op jit(solution)/shard_map/shared/ppermute | solution.py:468
  34.6 1.2 %collective-permute-done = bf16[128,1024]{1,0:T(8,128)(2,1)S(1)} collective-permute-done((bf16[128,1024]{1,0:T(8,128)(2,1)S(1)}, bf16[128,1024]{1,0:T(8,128)(2,1)S(1)}, u32[]{:S(2)}, u32[]{:S(2)}) %collective-permute-start) | collective-permute-done | bytes 262176 | tf_op jit(solution)/shard_map/shared/ppermute | solution.py:468
  35.8 0.1 add_convert_fusion
  35.8 0.0 copy-start.4
  35.9 19.1 %all_to_all.44 = bf16[8,16,1024]{2,1,0:T(8,128)(2,1)S(1)} all-to-all(bf16[8,16,1024]{2,1,0:T(8,128)(2,1)S(1)} %bitcast.26), channel_id=1, replica_groups={{0,2,4,6,8,10,12,14},{1,3,5,7,9,11,13,15},{16,18,20,22,24,26,28,30},{17..., dimensions={0} | all-to-all | bytes 524288 | tf_op jit(solution)/shard_map/shared/all_to_all | solution.py:471
  54.9 0.1 shared.1
  55.1 12.2 %all_to_all.45 = bf16[8,16,1024]{2,1,0:T(8,128)(2,1)S(1)} all-to-all(bf16[8,16,1024]{2,1,0:T(8,128)(2,1)S(1)} %bitcast.16), channel_id=1, replica_groups={{0,2,4,6,8,10,12,14},{1,3,5,7,9,11,13,15},{16,18,20,22,24,26,28,30},{17..., dimensions={0} | all-to-all | bytes 524288 | tf_op jit(solution)/shard_map/output/all_to_all | solution.py:474
  67.3 3.2 %collective-permute-start.1 = (bf16[128,1024]{1,0:T(8,128)(2,1)S(1)}, bf16[128,1024]{1,0:T(8,128)(2,1)S(1)}, u32[]{:S(2)}, u32[]{:S(2)}) collective-permute-start(bf16[128,1024]{1,0:T(8,128)(2,1)S(1)} %bitcast.18), channel_id=1, source_target_pairs={{0,1},{1,0},{2,3},{3,2},{4,5},{5,4},{6,7},{7,6},{8,9},{9,8},{10,11... | collective-permute-start | bytes 786440 | tf_op jit(solution)/shard_map/output/ppermute | solution.py:475
  70.4 0.2 output.2.own_ref
  70.7 0.9 %collective-permute-done.1.shared_ref = bf16[128,1024]{1,0:T(8,128)(2,1)S(1)} collective-permute-done((bf16[128,1024]{1,0:T(8,128)(2,1)S(1)}, bf16[128,1024]{1,0:T(8,128)(2,1)S(1)}, u32[]{:S(2)}, u32[]{:S(2)}) %collective-permute-start.1) | collective-permute-done | bytes 262176 | tf_op jit(solution)/shard_map/output/ppermute | solution.py:475
  71.6 0.9 %output.3 = bf16[256,256]{1,0:T(8,128)(2,1)} custom-call(bf16[128,1024]{1,0:T(8,128)(2,1)S(1)} %collective-permute-done.1.shared_ref, bf16[1024,256]{1,0:T(8,128)(2,1)S(1)} %copy-done, bf16[128,256]{1,0:T(8,128)(2,1)S(1)} %output.2.own_ref), custom_call_target="tpu_custom_call" | custom-call | tf_op jit(solution)/shard_map/output/pallas_call | solution.py:483
  (21 shorter events, 0.0 us)
Async XLA Ops:
  0.0 0.7 copy-start.5
  0.7 0.9 %copy-start.2 = (bf16[256,256]{1,0:T(8,128)(2,1)S(1)}, bf16[256,256]{1,0:T(8,128)(2,1)}, u32[]{:S(2)}) copy-start(bf16[256,256]{1,0:T(8,128)(2,1)} %tokens_ref.3) | copy-start | bytes 393220
  2.8 7.8 %copy-start.3 = (bf16[256,256]{1,0:T(8,128)(2,1)S(1)}, bf16[256,256]{1,0:T(8,128)(2,1)}, u32[]{:S(2)}) copy-start(bf16[256,256]{1,0:T(8,128)(2,1)} %tokens_ref.3) | copy-start | bytes 393220
  2.8 7.8 %copy-start.6 = (f32[2,16,256]{2,1,0:T(8,128)S(1)}, f32[2,16,256]{2,1,0:T(8,128)}, u32[]{:S(2)}) copy-start(f32[2,16,256]{2,1,0:T(8,128)} %output_ref.1) | copy-start | bytes 98308
  2.8 7.8 %copy-start.7 = (f32[16,256]{1,0:T(8,128)S(1)}, f32[16,256]{1,0:T(8,128)}, u32[]{:S(2)}) copy-start(f32[16,256]{1,0:T(8,128)} %decay_ref.1) | copy-start | bytes 49156
  2.8 7.8 %copy-start.8 = (f32[16,256]{1,0:T(8,128)S(1)}, f32[16,256]{1,0:T(8,128)}, u32[]{:S(2)}) copy-start(f32[16,256]{1,0:T(8,128)} %angle_ref.1) | copy-start | bytes 49156
  2.8 7.8 %copy-start.9 = (f32[16,256]{1,0:T(8,128)S(1)}, f32[16,256]{1,0:T(8,128)}, u32[]{:S(2)}) copy-start(f32[16,256]{1,0:T(8,128)} %input_ref.1) | copy-start | bytes 49156
  2.8 7.8 %copy-start.11 = (f32[256]{0:T(256)S(1)}, f32[256]{0:T(256)}, u32[]{:S(2)}) copy-start(f32[256]{0:T(256)} %param.14) | copy-start | bytes 3076
  2.8 7.8 %copy-start.12 = (f32[256]{0:T(256)S(1)}, f32[256]{0:T(256)}, u32[]{:S(2)}) copy-start(f32[256]{0:T(256)} %param.15) | copy-start | bytes 3076
  2.8 14.6 %all-to-all-start = ((f32[16,8,256]{2,1,0:T(8,128)}), f32[16,8,256]{2,1,0:T(8,128)S(1)}, u32[]{:S(2)}, u32[]{:S(2)}) async-start(f32[16,8,256]{2,1,0:T(8,128)} %bitcast.1), calls=%async_computation | async-start | bytes 262144 | tf_op jit(solution)/shard_map/stats/all_to_all | solution.py:419
  10.6 0.7 copy-start.10
  19.4 10.9 %all-to-all-start.1 = ((bf16[16,32,256]{2,1,0:T(8,128)(2,1)}), bf16[16,32,256]{2,1,0:T(8,128)(2,1)S(1)}, u32[]{:S(2)}, u32[]{:S(2)}) async-start(bf16[16,32,256]{2,1,0:T(8,128)(2,1)} %bitcast.6), calls=%async_computation.1 | async-start | bytes 524288 | tf_op jit(solution)/shard_map/local/all_to_all | solution.py:449
  23.0 7.3 %copy-start.1 = (bf16[256,1024]{1,0:T(8,128)(2,1)S(1)}, bf16[256,1024]{1,0:T(8,128)(2,1)}, u32[]{:S(2)}) copy-start(bf16[256,1024]{1,0:T(8,128)(2,1)} %weight_ref.3) | copy-start | bytes 1572868
  31.4 4.4 %collective-permute-start = (bf16[128,1024]{1,0:T(8,128)(2,1)S(1)}, bf16[128,1024]{1,0:T(8,128)(2,1)S(1)}, u32[]{:S(2)}, u32[]{:S(2)}) collective-permute-start(bf16[128,1024]{1,0:T(8,128)(2,1)S(1)} %get-tuple-element.29), channel_id=1, source_target_pairs={{0,1},{1,0},{2,3},{3,2},{4,5},{5,4},{6,7},{7,6},{8,9},{9,8},{10,11... | collective-permute-start | bytes 786440 | tf_op jit(solution)/shard_map/shared/ppermute | solution.py:468
  35.8 19.1 %copy-start.4 = (f32[1024]{0:T(1024)S(1)}, f32[1024]{0:T(1024)}, u32[]{:S(2)}) copy-start(f32[1024]{0:T(1024)} %param.22) | copy-start | bytes 12292
  54.9 15.5 %copy-start = (bf16[1024,256]{1,0:T(8,128)(2,1)S(1)}, bf16[1024,256]{1,0:T(8,128)(2,1)}, u32[]{:S(2)}) copy-start(bf16[1024,256]{1,0:T(8,128)(2,1)} %weight_ref.5) | copy-start | bytes 1572868
  67.3 4.3 %collective-permute-start.1 = (bf16[128,1024]{1,0:T(8,128)(2,1)S(1)}, bf16[128,1024]{1,0:T(8,128)(2,1)S(1)}, u32[]{:S(2)}, u32[]{:S(2)}) collective-permute-start(bf16[128,1024]{1,0:T(8,128)(2,1)S(1)} %bitcast.18), channel_id=1, source_target_pairs={{0,1},{1,0},{2,3},{3,2},{4,5},{5,4},{6,7},{7,6},{8,9},{9,8},{10,11... | collective-permute-start | bytes 786440 | tf_op jit(solution)/shard_map/output/ppermute | solution.py:475

commit v5 on v4

--- a/solution.py
+++ b/solution.py
@@ -23,6 +23,7 @@
 f32 = jnp.float32
 bf16 = jnp.bfloat16
 VMEM = pl.BlockSpec(memory_space=pltpu.VMEM)
+HBM = pl.BlockSpec(memory_space=pltpu.HBM)
 
 
 def dot(a, b):
@@ -41,19 +42,33 @@
     return jnp.where(mask, 1.0, 0.0).astype(bf16)
 
 
+def group_matrix():
+    return as_bf16(iota2((WIDTH, WIDTH), 0) // GROUP == iota2((WIDTH, WIDTH), 1) // GROUP)
+
+
 def dot_parts(a, b):
-    high = a.astype(bf16)
-    rest = a - high.astype(f32)
-    middle = rest.astype(bf16)
-    low = (rest - middle.astype(f32)).astype(bf16)
-    return dot(high, b) + dot(middle, b) + dot(low, b)
+    rows = a.shape[0]
+    high = a.astype(bf16).astype(f32)
+    rest = a - high
+    middle = rest.astype(bf16).astype(f32)
+    parts = jnp.concatenate([high, middle, rest - middle], axis=0).astype(bf16)
+    product = dot(parts, b)
+    return product[:rows] + product[rows : 2 * rows] + product[2 * rows :]
 
 
 def cmul(ar, ai, br, bi):
     return ar * br - ai * bi, ar * bi + ai * br
 
 
-def stats_kernel(tokens_ref, retain_ref, out_ref):
+def stats_kernel(tokens_hbm, retain_hbm, out_ref, tokens_ref, retain_ref, arrived):
+    copies = (
+        pltpu.make_async_copy(tokens_hbm, tokens_ref, arrived.at[0]),
+        pltpu.make_async_copy(retain_hbm, retain_ref, arrived.at[1]),
+    )
+    for copy in copies:
+        copy.start()
+    for copy in copies:
+        copy.wait()
     values = tokens_ref[...].astype(f32)
     total = jnp.sum(values, axis=0, keepdims=True)
     squares = jnp.sum(values * values, axis=0, keepdims=True)
@@ -96,8 +111,9 @@
     squares = values * values
     high = squares.astype(bf16)
     low = (squares - high.astype(f32)).astype(bf16)
-    sums_ref[...] = dot(upto, tokens)
-    squares_ref[...] = dot(upto, high) + dot(upto, low)
+    groups = group_matrix()
+    sums_ref[...] = dot_parts(dot(upto, tokens), groups)
+    squares_ref[...] = dot_parts(dot(upto, high) + dot(upto, low), groups)
     placed_ref[...] = dot(as_bf16(column == row), tokens)
 
     factor = jnp.sum(jnp.where(column == row, retain_ref[...], 0.0), axis=1, keepdims=True)
@@ -173,6 +189,7 @@
     power_ref,
     message_ref,
     scaled_ref,
+    ends_ref,
     summary,
 ):
     me = lax.axis_index("span")
@@ -180,9 +197,9 @@
     for i in range(SPANS):
         before += jnp.where(i < me, stats_ref[8 * i : 8 * i + 8, :], 0.0)
 
-    groups = as_bf16(iota2((WIDTH, WIDTH), 0) // GROUP == iota2((WIDTH, WIDTH), 1) // GROUP)
-    cum_sum = dot_parts(sums_ref[...] + before[0:1], groups)
-    cum_sq = dot_parts(squares_ref[...] + before[1:2], groups)
+    before = dot_parts(before, group_matrix())
+    cum_sum = sums_ref[...] + before[0:1]
+    cum_sq = squares_ref[...] + before[1:2]
     position = time_of(iota2((LENGTH, WIDTH), 0)) + me * LENGTH + 1
     share = 1.0 / (position * GROUP).astype(f32)
     average = cum_sum * share
@@ -206,6 +223,8 @@
                     ends[n] = ends[n] + u * power_ref[place : place + 1, lanes]
             for n in range(CHUNK):
                 j = first + n
+                ends_ref[16 * j : 16 * j + 8, lanes] = ends[n]
+                ends_ref[16 * j + 8 : 16 * j + 16, lanes] = ends[CHUNK + n]
                 end_re, end_im = cmul(
                     ends[n],
                     ends[CHUNK + n],
@@ -219,7 +238,7 @@
         message_ref[32 * i : 32 * i + 32, :] = sent
 
 
-def within_kernel(scaled_ref, retained_ref, pack_ref, mixed):
+def within_kernel(scaled_ref, ends_ref, retained_ref, pack_ref, mixed):
     block = iota2((BLOCKS, HALF), 0)
     running = retained_ref[LENGTH - BLOCKS : LENGTH, :]
     spans = [running]
@@ -239,24 +258,10 @@
             re_of = [wide(j, lanes) for j in js]
             im_of = [wide(16 + j, lanes) for j in js]
 
-            def end_on(step, held):
-                u = scaled_ref[pl.ds(pl.multiple_of(step * BLOCKS, BLOCKS), BLOCKS), lanes]
-                following = []
-                for n in range(CHUNK):
-                    re, im = held[2 * n], held[2 * n + 1]
-                    following.append(re * re_of[n] - im * im_of[n] + u)
-                    following.append(re * im_of[n] + im * re_of[n])
-                return tuple(following)
-
-            u0 = scaled_ref[0:BLOCKS, lanes]
-            u1 = scaled_ref[BLOCKS : 2 * BLOCKS, lanes]
-            begin = []
-            for n in range(CHUNK):
-                begin += [u0 * re_of[n] + u1, u0 * im_of[n]]
-            ends = lax.fori_loop(2, STEPS, end_on, tuple(begin), unroll=3)
             begin = []
             for n, j in enumerate(js):
-                re, im = running * ends[2 * n], running * ends[2 * n + 1]
+                re = running * ends_ref[16 * j : 16 * j + 8, lanes]
+                im = running * ends_ref[16 * j + 8 : 16 * j + 16, lanes]
                 for k in range(3):
                     add_re, add_im = cmul(
                         pltpu.roll(re, 2**k, 0),
@@ -369,15 +374,28 @@
         out_ref[16 * i : 16 * i + 16, :] = normed
 
 
-def own_kernel(shared_ref, weight_ref, out_ref):
-    out_ref[...] = dot(shared_ref[...], weight_ref[...]).astype(bf16)
-
-
-def other_kernel(shared_ref, weight_ref, own_ref, out_ref):
+def half_kernel(own, shared_ref, weight_ref, *refs):
+    out_ref, half, done = refs[-3:]
     core = lax.axis_index("tensor") % 2
-    other = dot(shared_ref[...], weight_ref[...]).astype(bf16)
-    out_ref[pl.ds(pl.multiple_of(core * HALF, HALF), HALF), :] = own_ref[...]
-    out_ref[pl.ds(pl.multiple_of((1 - core) * HALF, HALF), HALF), :] = other
+    side = core if own else 1 - core
+    place = pl.multiple_of(side * HALF, HALF)
+    half[...] = dot(shared_ref[...], weight_ref[...]).astype(bf16)
+    copy = pltpu.make_async_copy(half, out_ref.at[pl.ds(place, HALF), :], done)
+    copy.start()
+    copy.wait()
+
+
+def half_call(own, *operands):
+    return pl.pallas_call(
+        functools.partial(half_kernel, own),
+        out_shape=jax.ShapeDtypeStruct((LENGTH, WIDTH), bf16),
+        in_specs=[VMEM, VMEM] + [HBM] * (len(operands) - 2),
+        out_specs=HBM,
+        scratch_shapes=[pltpu.VMEM((HALF, WIDTH), bf16), pltpu.SemaphoreType.DMA],
+        input_output_aliases={} if own else {2: 0},
+        compiler_params=pltpu.CompilerParams(vmem_limit_bytes=16 * 2**20),
+        cost_estimate=pl.CostEstimate(flops=10**9, bytes_accessed=2**20, transcendentals=0),
+    )(*operands)
 
 
 def call(kernel, count, shapes, scratch=(), space=VMEM, limit=32, cost=None):
@@ -414,7 +432,13 @@
             stats_kernel,
             2,
             [((8 * SPANS, WIDTH), f32)],
-            limit=16,
+            [
+                pltpu.VMEM((LENGTH, WIDTH), bf16),
+                pltpu.VMEM((1, LENGTH), f32),
+                pltpu.SemaphoreType.DMA((2,)),
+            ],
+            HBM,
+            60,
         )(tokens, retain)
         stats = lax.all_to_all(own, "span", 0, 0, tiled=True)
     with jax.named_scope("local"):
@@ -439,21 +463,25 @@
             norm_gain.reshape(1, WIDTH),
             norm_bias.reshape(1, WIDTH),
         )
-        message, scaled = call(
+        message, scaled, ends = call(
             local_kernel,
             8,
-            [((32 * SPANS, WIDTH), bf16), ((LENGTH, WIDTH), f32)],
+            [
+                ((32 * SPANS, WIDTH), bf16),
+                ((LENGTH, WIDTH), f32),
+                ((2 * NDIM * BLOCKS, WIDTH), f32),
+            ],
             [pltpu.VMEM((32, WIDTH), f32)],
             limit=16,
         )(stats, sums, squares, placed, back, pack, leave, power)
         message = lax.all_to_all(message, "span", 0, 0, tiled=True)
         mixed = call(
             within_kernel,
-            3,
+            4,
             [((LENGTH, WIDTH), f32)],
             limit=16,
             cost=pl.CostEstimate(flops=2 * 10**9, bytes_accessed=2**22, transcendentals=0),
-        )(scaled, retained, pack)
+        )(scaled, ends, retained, pack)
     with jax.named_scope("finish"):
         width = shared_weight.shape[1]
         give, keep = call(
@@ -473,16 +501,8 @@
     with jax.named_scope("output"):
         half = lax.all_to_all(copies, "tensor", 0, 0, tiled=True, axis_index_groups=groups)
         other = lax.ppermute(half, "tensor", swap)
-        own = call(
-            own_kernel,
-            2,
-            [((HALF, WIDTH), bf16)],
-            limit=16,
-            cost=pl.CostEstimate(flops=10**9, bytes_accessed=2**20, transcendentals=0),
-        )(half, output_weight)
-        return call(other_kernel, 3, [((LENGTH, WIDTH), bf16)], limit=16)(
-            other, output_weight, own
-        )
+        out = half_call(True, half, output_weight)
+        return half_call(False, other, output_weight, out)
 
 
 def solution(mesh):

time: 72.9 us -> 72 us (0.988)
  local copies, waits for them, and re-layouts: 2.24 us -> 0.66 us
    unnamed x26 -> x24, local copies, waits for them, and re-layouts: 2.24 us -> 0.66 us
    all_to_all x1, waiting for transfers between devices: 4.08 us -> 5.11 us  [shards(): message = lax.all_to_all(message, 'span', 0, 0, tiled=True)]
where the time goes in v5:
time: 72 us; the launch traced here: 71.6 us
  blocking collectives  31.3 us (43%)
  starting transfers between devices  17.7 us (25%)
  waiting for transfers between devices  11.8 us (16%)
  Pallas kernels  9.86 us (14%)
    all_to_all x1, blocking collectives, shards(): lax.all_to_all(pair, 'tensor', 0, 0, tiled=True, axis_index_groups=groups)  19.1 us
    all_to_all x1, blocking collectives, shards(): lax.all_to_all(copies, 'tensor', 0, 0, tiled=True, axis_index_groups=groups)  12.2 us
    all_to_all x1, starting transfers between devices, shards(): stats = lax.all_to_all(own, 'span', 0, 0, tiled=True)  7.73 us
    all_to_all x1, waiting for transfers between devices, shards(): stats = lax.all_to_all(own, 'span', 0, 0, tiled=True)  5.3 us
    all_to_all x1, waiting for transfers between devices, shards(): message = lax.all_to_all(message, 'span', 0, 0, tiled=True)  5.11 us
    all_to_all x1, starting transfers between devices, shards(): message = lax.all_to_all(message, 'span', 0, 0, tiled=True)  3.53 us
    ppermute x1, starting transfers between devices, shards(): taken = lax.ppermute(give, 'tensor', swap)  3.23 us
    ppermute x1, starting transfers between devices, shards(): other = lax.ppermute(half, 'tensor', swap)  3.17 us
  transfers between devices with their start and end apart: 4, of which 4 were waited for; matrix products, arithmetic and copies ran while one was open for 0% of the time, Pallas kernels for 6%

profile of v5, /device:TPU:1, one launch (start us, length us, event | category | flops | bytes accessed | tf_op | source)
XLA Modules:
  0.0 71.6 jit_solution(15004724606073014541)
XLA Ops:
  0.0 2.1 %stats.1 = f32[128,256]{1,0:T(8,128)} custom-call(bf16[256,256]{1,0:T(8,128)(2,1)} %tokens_ref.1, f32[1,256]{1,0:T(1,128)} %bitcast.21), custom_call_target="tpu_custom_call" | custom-call | tf_op jit(solution)/shard_map/stats/pallas_call | solution.py:431
  2.1 0.0 copy-start.1
  2.2 0.0 copy-start.7
  2.2 0.0 copy-start.8
  2.2 0.0 copy-start.11
  2.2 7.7 %all-to-all-start = ((f32[16,8,256]{2,1,0:T(8,128)}), f32[16,8,256]{2,1,0:T(8,128)S(1)}, u32[]{:S(2)}, u32[]{:S(2)}) async-start(f32[16,8,256]{2,1,0:T(8,128)} %bitcast.27), calls=%async_computation | async-start | bytes 262144 | tf_op jit(solution)/shard_map/stats/all_to_all | solution.py:443
  10.1 0.6 copy-done.3
  10.7 0.9 %local.3 = (f32[256,256]{1,0:T(8,128)S(1)}, f32[256,256]{1,0:T(8,128)S(1)}, f32[256,256]{1,0:T(8,128)S(1)}, f32[256,128]{1,0:T(8,128)S(1)}, f32[256,128]{1,0:T(8...) custom-call(bf16[256,256]{1,0:T(8,128)(2,1)S(1)} %copy-done.1, ...), custom_call_target="tpu_custom_call" | custom-call | flops 2000000000 | bytes 4194304 | tf_op jit(solution)/shard_map/local/pallas_call | solution.py:445
  11.5 5.3 %all-to-all-done = f32[16,8,256]{2,1,0:T(8,128)S(1)} async-done(((f32[16,8,256]{2,1,0:T(8,128)}), f32[16,8,256]{2,1,0:T(8,128)S(1)}, u32[]{:S(2)}, u32[]{:S(2)}) %all-to-all-start) | async-done | bytes 131104 | tf_op jit(solution)/shard_map/stats/all_to_all | solution.py:443
  16.8 1.7 %local.4 = (bf16[512,256]{1,0:T(8,128)(2,1)}, f32[256,256]{1,0:T(8,128)S(1)}, f32[256,256]{1,0:T(8,128)S(1)}) custom-call(f32[128,256]{1,0:T(8,128)S(1)} %bitcast.13, f32[256,256]{1,0:T(8,128)S(1)} %get-tuple-element.19.sums_ref, f32[256,256]{1,0:T(8,128)S(1)} %get-tuple-element.20.squares_ref, f32[256,256]{1,0:T(8,128)S(1)} %get-tuple-element.21.placed_ref, ...), custom_call_target="tpu_custom_call" | custom-call | tf_op jit(solution)/shard_map/local/pallas_call | solution.py:466
  18.5 3.5 %all-to-all-start.1 = ((bf16[16,32,256]{2,1,0:T(8,128)(2,1)}), bf16[16,32,256]{2,1,0:T(8,128)(2,1)S(1)}, u32[]{:S(2)}, u32[]{:S(2)}) async-start(bf16[16,32,256]{2,1,0:T(8,128)(2,1)} %bitcast.6), calls=%async_computation.1 | async-start | bytes 524288 | tf_op jit(solution)/shard_map/local/all_to_all | solution.py:477
  22.1 2.2 %local.5.mixed_ref = f32[256,256]{1,0:T(8,128)S(1)} custom-call(f32[256,256]{1,0:T(8,128)S(1)} %get-tuple-element.27.scaled_ref, f32[256,256]{1,0:T(8,128)S(1)} %get-tuple-element.28.ends_ref, f32[256,128]{1,0:T(8,128)S(1)} %get-tuple-element.29.retained_ref, f32[216,256]{1,0:T(8,128)S(1)} %get-tuple-element.23.pack_ref), custom_call_target="tpu_custom_call" | custom-call | flops 2000000000 | bytes 4194304 | tf_op jit(solution)/shard_map/local/pallas_call | solution.py:478
  24.3 5.1 %all-to-all-done.1 = bf16[16,32,256]{2,1,0:T(8,128)(2,1)S(1)} async-done(((bf16[16,32,256]{2,1,0:T(8,128)(2,1)}), bf16[16,32,256]{2,1,0:T(8,128)(2,1)S(1)}, u32[]{:S(2)}, u32[]{:S(2)}) %all-to-all-start.1) | async-done | bytes 262176 | tf_op jit(solution)/shard_map/local/all_to_all | solution.py:477
  29.4 1.1 %finish.1 = (bf16[128,1024]{1,0:T(8,128)(2,1)S(1)}, bf16[128,1024]{1,0:T(8,128)(2,1)S(1)}) custom-call(bf16[512,256]{1,0:T(8,128)(2,1)S(1)} %bitcast.17, f32[128,256]{1,0:T(8,128)S(1)} %bitcast.14, f32[256,256]{1,0:T(8,128)S(1)} %local.5.mixed_ref, f32[256,128]{1,0:T(8,128)S(1)} %get-tuple-element.29.retained_ref, ...), custom_call_target="tpu_custom_call" | custom-call | tf_op jit(solution)/shard_map/finish/pallas_call | solution.py:487
  30.5 3.2 %collective-permute-start = (bf16[128,1024]{1,0:T(8,128)(2,1)S(1)}, bf16[128,1024]{1,0:T(8,128)(2,1)S(1)}, u32[]{:S(2)}, u32[]{:S(2)}) collective-permute-start(bf16[128,1024]{1,0:T(8,128)(2,1)S(1)} %get-tuple-element.31), channel_id=1, source_target_pairs={{0,1},{1,0},{2,3},{3,2},{4,5},{5,4},{6,7},{7,6},{8,9},{9,8},{10,11... | collective-permute-start | bytes 786440 | tf_op jit(solution)/shard_map/shared/ppermute | solution.py:496
  33.7 1.2 %collective-permute-done = bf16[128,1024]{1,0:T(8,128)(2,1)S(1)} collective-permute-done((bf16[128,1024]{1,0:T(8,128)(2,1)S(1)}, bf16[128,1024]{1,0:T(8,128)(2,1)S(1)}, u32[]{:S(2)}, u32[]{:S(2)}) %collective-permute-start) | collective-permute-done | bytes 262176 | tf_op jit(solution)/shard_map/shared/ppermute | solution.py:496
  34.9 0.1 add_convert_fusion
  35.0 19.1 %all_to_all.44 = bf16[8,16,1024]{2,1,0:T(8,128)(2,1)S(1)} all-to-all(bf16[8,16,1024]{2,1,0:T(8,128)(2,1)S(1)} %bitcast.26), channel_id=1, replica_groups={{0,2,4,6,8,10,12,14},{1,3,5,7,9,11,13,15},{16,18,20,22,24,26,28,30},{17..., dimensions={0} | all-to-all | bytes 524288 | tf_op jit(solution)/shard_map/shared/all_to_all | solution.py:499
  54.0 0.1 shared.1
  54.2 12.2 %all_to_all.45 = bf16[8,16,1024]{2,1,0:T(8,128)(2,1)S(1)} all-to-all(bf16[8,16,1024]{2,1,0:T(8,128)(2,1)S(1)} %bitcast.16), channel_id=1, replica_groups={{0,2,4,6,8,10,12,14},{1,3,5,7,9,11,13,15},{16,18,20,22,24,26,28,30},{17..., dimensions={0} | all-to-all | bytes 524288 | tf_op jit(solution)/shard_map/output/all_to_all | solution.py:502
  66.4 3.2 %collective-permute-start.1 = (bf16[128,1024]{1,0:T(8,128)(2,1)S(1)}, bf16[128,1024]{1,0:T(8,128)(2,1)S(1)}, u32[]{:S(2)}, u32[]{:S(2)}) collective-permute-start(bf16[128,1024]{1,0:T(8,128)(2,1)S(1)} %bitcast.18), channel_id=1, source_target_pairs={{0,1},{1,0},{2,3},{3,2},{4,5},{5,4},{6,7},{7,6},{8,9},{9,8},{10,11... | collective-permute-start | bytes 786440 | tf_op jit(solution)/shard_map/output/ppermute | solution.py:503
  69.5 0.9 %output.2.refs_0_ = bf16[256,256]{1,0:T(8,128)(2,1)} custom-call(bf16[128,1024]{1,0:T(8,128)(2,1)S(1)} %bitcast.19, bf16[1024,256]{1,0:T(8,128)(2,1)S(1)} %copy-done.4), custom_call_target="tpu_custom_call" | custom-call | flops 1000000000 | bytes 1048576 | tf_op jit(solution)/shard_map/output/pallas_call | solution.py:389
  70.4 0.3 collective-permute-done.1.shared_ref
  70.7 0.9 %output.3 = bf16[256,256]{1,0:T(8,128)(2,1)} custom-call(bf16[128,1024]{1,0:T(8,128)(2,1)S(1)} %collective-permute-done.1.shared_ref, bf16[1024,256]{1,0:T(8,128)(2,1)S(1)} %copy-done.4, bf16[256,256]{1,0:T(8,128)(2,1)} %output.2.refs_0_), custom_call_target="tpu_custom_call", output_to_operand_aliasing={{}: (2, {})} | custom-call | flops 1000000000 | bytes 1048576 | tf_op jit(solution)/shard_map/output/pallas_call | solution.py:389
  (19 shorter events, 0.1 us)
Async XLA Ops:
  2.1 7.8 %copy-start.1 = (bf16[256,256]{1,0:T(8,128)(2,1)S(1)}, bf16[256,256]{1,0:T(8,128)(2,1)}, u32[]{:S(2)}) copy-start(bf16[256,256]{1,0:T(8,128)(2,1)} %tokens_ref.1) | copy-start | bytes 393220
  2.2 7.8 %copy-start.5 = (f32[2,16,256]{2,1,0:T(8,128)S(1)}, f32[2,16,256]{2,1,0:T(8,128)}, u32[]{:S(2)}) copy-start(f32[2,16,256]{2,1,0:T(8,128)} %output_ref.1) | copy-start | bytes 98308
  2.2 7.8 %copy-start.6 = (f32[16,256]{1,0:T(8,128)S(1)}, f32[16,256]{1,0:T(8,128)}, u32[]{:S(2)}) copy-start(f32[16,256]{1,0:T(8,128)} %decay_ref.1) | copy-start | bytes 49156
  2.2 7.8 %copy-start.7 = (f32[16,256]{1,0:T(8,128)S(1)}, f32[16,256]{1,0:T(8,128)}, u32[]{:S(2)}) copy-start(f32[16,256]{1,0:T(8,128)} %angle_ref.1) | copy-start | bytes 49156
  2.2 7.8 %copy-start.8 = (f32[16,256]{1,0:T(8,128)S(1)}, f32[16,256]{1,0:T(8,128)}, u32[]{:S(2)}) copy-start(f32[16,256]{1,0:T(8,128)} %input_ref.1) | copy-start | bytes 49156
  2.2 7.8 %copy-start.9 = (f32[256]{0:T(256)S(1)}, f32[256]{0:T(256)}, u32[]{:S(2)}) copy-start(f32[256]{0:T(256)} %param.20) | copy-start | bytes 3076
  2.2 7.8 %copy-start.10 = (f32[256]{0:T(256)S(1)}, f32[256]{0:T(256)}, u32[]{:S(2)}) copy-start(f32[256]{0:T(256)} %param.14) | copy-start | bytes 3076
  2.2 7.8 %copy-start.11 = (f32[256]{0:T(256)S(1)}, f32[256]{0:T(256)}, u32[]{:S(2)}) copy-start(f32[256]{0:T(256)} %param.15) | copy-start | bytes 3076
  2.2 14.6 %all-to-all-start = ((f32[16,8,256]{2,1,0:T(8,128)}), f32[16,8,256]{2,1,0:T(8,128)S(1)}, u32[]{:S(2)}, u32[]{:S(2)}) async-start(f32[16,8,256]{2,1,0:T(8,128)} %bitcast.27), calls=%async_computation | async-start | bytes 262144 | tf_op jit(solution)/shard_map/stats/all_to_all | solution.py:443
  10.0 0.7 copy-start.3
  18.5 10.9 %all-to-all-start.1 = ((bf16[16,32,256]{2,1,0:T(8,128)(2,1)}), bf16[16,32,256]{2,1,0:T(8,128)(2,1)S(1)}, u32[]{:S(2)}, u32[]{:S(2)}) async-start(bf16[16,32,256]{2,1,0:T(8,128)(2,1)} %bitcast.6), calls=%async_computation.1 | async-start | bytes 524288 | tf_op jit(solution)/shard_map/local/all_to_all | solution.py:477
  22.1 7.3 %copy-start = (bf16[256,1024]{1,0:T(8,128)(2,1)S(1)}, bf16[256,1024]{1,0:T(8,128)(2,1)}, u32[]{:S(2)}) copy-start(bf16[256,1024]{1,0:T(8,128)(2,1)} %weight_ref.3) | copy-start | bytes 1572868
  30.5 4.4 %collective-permute-start = (bf16[128,1024]{1,0:T(8,128)(2,1)S(1)}, bf16[128,1024]{1,0:T(8,128)(2,1)S(1)}, u32[]{:S(2)}, u32[]{:S(2)}) collective-permute-start(bf16[128,1024]{1,0:T(8,128)(2,1)S(1)} %get-tuple-element.31), channel_id=1, source_target_pairs={{0,1},{1,0},{2,3},{3,2},{4,5},{5,4},{6,7},{7,6},{8,9},{9,8},{10,11... | collective-permute-start | bytes 786440 | tf_op jit(solution)/shard_map/shared/ppermute | solution.py:496
  34.9 19.1 %copy-start.2 = (f32[1024]{0:T(1024)S(1)}, f32[1024]{0:T(1024)}, u32[]{:S(2)}) copy-start(f32[1024]{0:T(1024)} %param.22) | copy-start | bytes 12292
  54.0 15.5 %copy-start.4 = (bf16[1024,256]{1,0:T(8,128)(2,1)S(1)}, bf16[1024,256]{1,0:T(8,128)(2,1)}, u32[]{:S(2)}) copy-start(bf16[1024,256]{1,0:T(8,128)(2,1)} %weight_ref.5) | copy-start | bytes 1572868
  66.4 4.3 %collective-permute-start.1 = (bf16[128,1024]{1,0:T(8,128)(2,1)S(1)}, bf16[128,1024]{1,0:T(8,128)(2,1)S(1)}, u32[]{:S(2)}, u32[]{:S(2)}) collective-permute-start(bf16[128,1024]{1,0:T(8,128)(2,1)S(1)} %bitcast.18), channel_id=1, source_target_pairs={{0,1},{1,0},{2,3},{3,2},{4,5},{5,4},{6,7},{7,6},{8,9},{9,8},{10,11... | collective-permute-start | bytes 786440 | tf_op jit(solution)/shard_map/output/ppermute | solution.py:503

commit v6 on v5

--- a/solution.py
+++ b/solution.py
@@ -61,22 +61,28 @@
 
 
 def stats_kernel(tokens_hbm, retain_hbm, out_ref, tokens_ref, retain_ref, arrived):
-    copies = (
-        pltpu.make_async_copy(tokens_hbm, tokens_ref, arrived.at[0]),
-        pltpu.make_async_copy(retain_hbm, retain_ref, arrived.at[1]),
-    )
+    pieces = 4
+    size = LENGTH // pieces
+    copies = [pltpu.make_async_copy(retain_hbm, retain_ref, arrived.at[pieces])]
+    for i in range(pieces):
+        rows = pl.ds(i * size, size)
+        copies.append(
+            pltpu.make_async_copy(tokens_hbm.at[rows, :], tokens_ref.at[rows, :], arrived.at[i])
+        )
     for copy in copies:
         copy.start()
-    for copy in copies:
-        copy.wait()
-    values = tokens_ref[...].astype(f32)
-    total = jnp.sum(values, axis=0, keepdims=True)
-    squares = jnp.sum(values * values, axis=0, keepdims=True)
+    copies[0].wait()
     kept = retain_ref[...]
-    size = LENGTH
-    while size > 1:
-        size //= 2
-        kept = kept[:, :size] * kept[:, size:]
+    kept = kept[:, :HALF] * kept[:, HALF:]
+    for k in range(7):
+        kept = kept * pltpu.roll(kept, 2**k, 1)
+    kept = jnp.concatenate([kept, kept], axis=1)
+    total = squares = 0.0
+    for i in range(pieces):
+        copies[1 + i].wait()
+        values = tokens_ref[size * i : size * i + size, :].astype(f32)
+        total = total + jnp.sum(values, axis=0, keepdims=True)
+        squares = squares + jnp.sum(values * values, axis=0, keepdims=True)
     row = iota2((8, WIDTH), 0)
     block = jnp.where(row == 0, total, jnp.where(row == 1, squares, kept))
     for i in range(SPANS):
@@ -308,7 +314,7 @@
     power_ref,
     weight_ref,
     give_ref,
-    keep_ref,
+    active_ref,
     entering,
     mixed,
 ):
@@ -355,13 +361,19 @@
     retained = retained_ref[...]
     ema = jnp.concatenate([retained, retained], axis=1) * mixed[...]
     active = (ema / (1.0 + jnp.exp(-ema))).astype(bf16)
-    slot = iota2((LENGTH, LENGTH), 0)
-    wanted = (slot + (1 - core) * HALF) % LENGTH
-    chosen = as_bf16(time_of(iota2((LENGTH, LENGTH), 1)) == wanted)
-    ordered = dot(chosen, active).astype(bf16)
-    product = dot(ordered, weight_ref[...]).astype(bf16)
-    give_ref[...] = product[:HALF]
-    keep_ref[...] = product[HALF:]
+    active_ref[...] = active
+    give_ref[...] = half_product(1 - core, active, weight_ref[...])
+
+
+def half_product(side, active, weight):
+    wanted = iota2((HALF, LENGTH), 0) + side * HALF
+    chosen = as_bf16(time_of(iota2((HALF, LENGTH), 1)) == wanted)
+    return dot(dot(chosen, active).astype(bf16), weight).astype(bf16)
+
+
+def keep_kernel(active_ref, weight_ref, keep_ref):
+    core = lax.axis_index("tensor") % 2
+    keep_ref[...] = half_product(core, active_ref[...], weight_ref[...])
 
 
 def norm_kernel(parts_ref, gain_ref, out_ref):
@@ -435,7 +447,7 @@
             [
                 pltpu.VMEM((LENGTH, WIDTH), bf16),
                 pltpu.VMEM((1, LENGTH), f32),
-                pltpu.SemaphoreType.DMA((2,)),
+                pltpu.SemaphoreType.DMA((5,)),
             ],
             HBM,
             60,
@@ -484,16 +496,23 @@
         )(scaled, ends, retained, pack)
     with jax.named_scope("finish"):
         width = shared_weight.shape[1]
-        give, keep = call(
+        give, active = call(
             finish_kernel,
             8,
-            [((HALF, width), bf16), ((HALF, width), bf16)],
+            [((HALF, width), bf16), ((LENGTH, WIDTH), bf16)],
             [pltpu.VMEM((32, WIDTH), f32), pltpu.VMEM((LENGTH, WIDTH), f32)],
             limit=16,
         )(message, stats, mixed, retained, pack, enter, power, shared_weight)
     with jax.named_scope("shared"):
         swap = [(i, i ^ 1) for i in range(16)]
         taken = lax.ppermute(give, "tensor", swap)
+        keep = call(
+            keep_kernel,
+            2,
+            [((HALF, width), bf16)],
+            limit=16,
+            cost=pl.CostEstimate(flops=10**9, bytes_accessed=2**20, transcendentals=0),
+        )(active, shared_weight)
         pair = (taken.astype(f32) + keep.astype(f32)).astype(bf16)
         groups = [[core + 2 * z for z in range(8)] for core in range(2)]
         parts = lax.all_to_all(pair, "tensor", 0, 0, tiled=True, axis_index_groups=groups)

time: 72 us -> 71.8 us (level)
  no operation moved by 1% of the time
where the time goes in v6:
time: 71.8 us; the launch traced here: 71.3 us
  blocking collectives  31.3 us (44%)
  starting transfers between devices  17.7 us (25%)
  waiting for transfers between devices  11.5 us (16%)
  Pallas kernels  9.98 us (14%)
    all_to_all x1, blocking collectives, shards(): lax.all_to_all(pair, 'tensor', 0, 0, tiled=True, axis_index_groups=groups)  19.1 us
    all_to_all x1, blocking collectives, shards(): lax.all_to_all(copies, 'tensor', 0, 0, tiled=True, axis_index_groups=groups)  12.2 us
    all_to_all x1, starting transfers between devices, shards(): stats = lax.all_to_all(own, 'span', 0, 0, tiled=True)  7.73 us
    all_to_all x1, waiting for transfers between devices, shards(): stats = lax.all_to_all(own, 'span', 0, 0, tiled=True)  5.3 us
    all_to_all x1, waiting for transfers between devices, shards(): message = lax.all_to_all(message, 'span', 0, 0, tiled=True)  5.11 us
    all_to_all x1, starting transfers between devices, shards(): message = lax.all_to_all(message, 'span', 0, 0, tiled=True)  3.53 us
    ppermute x1, starting transfers between devices, shards(): taken = lax.ppermute(give, 'tensor', swap)  3.23 us
    ppermute x1, starting transfers between devices, shards(): other = lax.ppermute(half, 'tensor', swap)  3.17 us
  transfers between devices with their start and end apart: 4, of which 4 were waited for; matrix products, arithmetic and copies ran while one was open for 0% of the time, Pallas kernels for 6%

profile of v6, /device:TPU:1, one launch (start us, length us, event | category | flops | bytes accessed | tf_op | source)
XLA Modules:
  0.0 71.3 jit_solution(872919311068626216)
XLA Ops:
  0.0 1.9 %stats.1 = f32[128,256]{1,0:T(8,128)} custom-call(bf16[256,256]{1,0:T(8,128)(2,1)} %tokens_ref.1, f32[1,256]{1,0:T(1,128)} %bitcast.21), custom_call_target="tpu_custom_call" | custom-call | tf_op jit(solution)/shard_map/stats/pallas_call | solution.py:443
  1.9 0.0 copy-start.1
  2.0 0.0 copy-start.5
  2.0 0.0 copy-start.8
  2.0 7.7 %all-to-all-start = ((f32[16,8,256]{2,1,0:T(8,128)}), f32[16,8,256]{2,1,0:T(8,128)S(1)}, u32[]{:S(2)}, u32[]{:S(2)}) async-start(f32[16,8,256]{2,1,0:T(8,128)} %bitcast.27), calls=%async_computation | async-start | bytes 262144 | tf_op jit(solution)/shard_map/stats/all_to_all | solution.py:455
  9.9 0.6 copy-done.3
  10.5 0.9 %local.3 = (f32[256,256]{1,0:T(8,128)S(1)}, f32[256,256]{1,0:T(8,128)S(1)}, f32[256,256]{1,0:T(8,128)S(1)}, f32[256,128]{1,0:T(8,128)S(1)}, f32[256,128]{1,0:T(8...) custom-call(bf16[256,256]{1,0:T(8,128)(2,1)S(1)} %copy-done.1, ...), custom_call_target="tpu_custom_call" | custom-call | flops 2000000000 | bytes 4194304 | tf_op jit(solution)/shard_map/local/pallas_call | solution.py:457
  11.3 5.3 %all-to-all-done = f32[16,8,256]{2,1,0:T(8,128)S(1)} async-done(((f32[16,8,256]{2,1,0:T(8,128)}), f32[16,8,256]{2,1,0:T(8,128)S(1)}, u32[]{:S(2)}, u32[]{:S(2)}) %all-to-all-start) | async-done | bytes 131104 | tf_op jit(solution)/shard_map/stats/all_to_all | solution.py:455
  16.6 1.7 %local.4 = (bf16[512,256]{1,0:T(8,128)(2,1)}, f32[256,256]{1,0:T(8,128)S(1)}, f32[256,256]{1,0:T(8,128)S(1)}) custom-call(f32[128,256]{1,0:T(8,128)S(1)} %bitcast.13, f32[256,256]{1,0:T(8,128)S(1)} %get-tuple-element.19.sums_ref, f32[256,256]{1,0:T(8,128)S(1)} %get-tuple-element.20.squares_ref, f32[256,256]{1,0:T(8,128)S(1)} %get-tuple-element.21.placed_ref, ...), custom_call_target="tpu_custom_call" | custom-call | tf_op jit(solution)/shard_map/local/pallas_call | solution.py:478
  18.3 3.5 %all-to-all-start.1 = ((bf16[16,32,256]{2,1,0:T(8,128)(2,1)}), bf16[16,32,256]{2,1,0:T(8,128)(2,1)S(1)}, u32[]{:S(2)}, u32[]{:S(2)}) async-start(bf16[16,32,256]{2,1,0:T(8,128)(2,1)} %bitcast.6), calls=%async_computation.1 | async-start | bytes 524288 | tf_op jit(solution)/shard_map/local/all_to_all | solution.py:489
  21.9 2.2 %local.5.mixed_ref = f32[256,256]{1,0:T(8,128)S(1)} custom-call(f32[256,256]{1,0:T(8,128)S(1)} %get-tuple-element.27.scaled_ref, f32[256,256]{1,0:T(8,128)S(1)} %get-tuple-element.28.ends_ref, f32[256,128]{1,0:T(8,128)S(1)} %get-tuple-element.29.retained_ref, f32[216,256]{1,0:T(8,128)S(1)} %get-tuple-element.23.pack_ref), custom_call_target="tpu_custom_call" | custom-call | flops 2000000000 | bytes 4194304 | tf_op jit(solution)/shard_map/local/pallas_call | solution.py:490
  24.1 5.1 %all-to-all-done.1 = bf16[16,32,256]{2,1,0:T(8,128)(2,1)S(1)} async-done(((bf16[16,32,256]{2,1,0:T(8,128)(2,1)}), bf16[16,32,256]{2,1,0:T(8,128)(2,1)S(1)}, u32[]{:S(2)}, u32[]{:S(2)}) %all-to-all-start.1) | async-done | bytes 262176 | tf_op jit(solution)/shard_map/local/all_to_all | solution.py:489
  29.2 1.0 %finish.1 = (bf16[128,1024]{1,0:T(8,128)(2,1)S(1)}, bf16[256,256]{1,0:T(8,128)(2,1)S(1)}) custom-call(bf16[512,256]{1,0:T(8,128)(2,1)S(1)} %bitcast.17, f32[128,256]{1,0:T(8,128)S(1)} %bitcast.14, f32[256,256]{1,0:T(8,128)S(1)} %local.5.mixed_ref, f32[256,128]{1,0:T(8,128)S(1)} %get-tuple-element.29.retained_ref, f32[216,256]{1,0:T(8,128)S(1)} %get-tuple-element.23.pack_ref, ...), custom_call_target="tpu_custom_call" | custom-call | tf_op jit(solution)/shard_map/finish/pallas_call | solution.py:499
  30.2 3.2 %collective-permute-start = (bf16[128,1024]{1,0:T(8,128)(2,1)S(1)}, bf16[128,1024]{1,0:T(8,128)(2,1)S(1)}, u32[]{:S(2)}, u32[]{:S(2)}) collective-permute-start(bf16[128,1024]{1,0:T(8,128)(2,1)S(1)} %get-tuple-element.31), channel_id=1, source_target_pairs={{0,1},{1,0},{2,3},{3,2},{4,5},{5,4},{6,7},{7,6},{8,9},{9,8},{10,11... | collective-permute-start | bytes 786440 | tf_op jit(solution)/shard_map/shared/ppermute | solution.py:508
  33.5 0.4 shared.2
  33.8 0.8 %collective-permute-done = bf16[128,1024]{1,0:T(8,128)(2,1)S(1)} collective-permute-done((bf16[128,1024]{1,0:T(8,128)(2,1)S(1)}, bf16[128,1024]{1,0:T(8,128)(2,1)S(1)}, u32[]{:S(2)}, u32[]{:S(2)}) %collective-permute-start) | collective-permute-done | bytes 262176 | tf_op jit(solution)/shard_map/shared/ppermute | solution.py:508
  34.6 0.1 add_convert_fusion
  34.7 19.1 %all_to_all.44 = bf16[8,16,1024]{2,1,0:T(8,128)(2,1)S(1)} all-to-all(bf16[8,16,1024]{2,1,0:T(8,128)(2,1)S(1)} %bitcast.26), channel_id=1, replica_groups={{0,2,4,6,8,10,12,14},{1,3,5,7,9,11,13,15},{16,18,20,22,24,26,28,30},{17..., dimensions={0} | all-to-all | bytes 524288 | tf_op jit(solution)/shard_map/shared/all_to_all | solution.py:518
  53.8 0.1 shared.3
  53.9 12.2 %all_to_all.45 = bf16[8,16,1024]{2,1,0:T(8,128)(2,1)S(1)} all-to-all(bf16[8,16,1024]{2,1,0:T(8,128)(2,1)S(1)} %bitcast.16), channel_id=1, replica_groups={{0,2,4,6,8,10,12,14},{1,3,5,7,9,11,13,15},{16,18,20,22,24,26,28,30},{17..., dimensions={0} | all-to-all | bytes 524288 | tf_op jit(solution)/shard_map/output/all_to_all | solution.py:521
  66.1 3.2 %collective-permute-start.1 = (bf16[128,1024]{1,0:T(8,128)(2,1)S(1)}, bf16[128,1024]{1,0:T(8,128)(2,1)S(1)}, u32[]{:S(2)}, u32[]{:S(2)}) collective-permute-start(bf16[128,1024]{1,0:T(8,128)(2,1)S(1)} %bitcast.18), channel_id=1, source_target_pairs={{0,1},{1,0},{2,3},{3,2},{4,5},{5,4},{6,7},{7,6},{8,9},{9,8},{10,11... | collective-permute-start | bytes 786440 | tf_op jit(solution)/shard_map/output/ppermute | solution.py:522
  69.3 0.9 %output.2.refs_0_ = bf16[256,256]{1,0:T(8,128)(2,1)} custom-call(bf16[128,1024]{1,0:T(8,128)(2,1)S(1)} %bitcast.19, bf16[1024,256]{1,0:T(8,128)(2,1)S(1)} %copy-done.4), custom_call_target="tpu_custom_call" | custom-call | flops 1000000000 | bytes 1048576 | tf_op jit(solution)/shard_map/output/pallas_call | solution.py:401
  70.2 0.3 collective-permute-done.1.shared_ref
  70.5 0.9 %output.3 = bf16[256,256]{1,0:T(8,128)(2,1)} custom-call(bf16[128,1024]{1,0:T(8,128)(2,1)S(1)} %collective-permute-done.1.shared_ref, bf16[1024,256]{1,0:T(8,128)(2,1)S(1)} %copy-done.4, bf16[256,256]{1,0:T(8,128)(2,1)} %output.2.refs_0_), custom_call_target="tpu_custom_call", output_to_operand_aliasing={{}: (2, {})} | custom-call | flops 1000000000 | bytes 1048576 | tf_op jit(solution)/shard_map/output/pallas_call | solution.py:401
  (20 shorter events, 0.1 us)
Async XLA Ops:
  1.9 7.8 %copy-start.1 = (bf16[256,256]{1,0:T(8,128)(2,1)S(1)}, bf16[256,256]{1,0:T(8,128)(2,1)}, u32[]{:S(2)}) copy-start(bf16[256,256]{1,0:T(8,128)(2,1)} %tokens_ref.1) | copy-start | bytes 393220
  2.0 7.8 %copy-start.5 = (f32[2,16,256]{2,1,0:T(8,128)S(1)}, f32[2,16,256]{2,1,0:T(8,128)}, u32[]{:S(2)}) copy-start(f32[2,16,256]{2,1,0:T(8,128)} %output_ref.1) | copy-start | bytes 98308
  2.0 7.8 %copy-start.6 = (f32[16,256]{1,0:T(8,128)S(1)}, f32[16,256]{1,0:T(8,128)}, u32[]{:S(2)}) copy-start(f32[16,256]{1,0:T(8,128)} %decay_ref.1) | copy-start | bytes 49156
  2.0 7.8 %copy-start.7 = (f32[16,256]{1,0:T(8,128)S(1)}, f32[16,256]{1,0:T(8,128)}, u32[]{:S(2)}) copy-start(f32[16,256]{1,0:T(8,128)} %angle_ref.1) | copy-start | bytes 49156
  2.0 7.8 %copy-start.8 = (f32[16,256]{1,0:T(8,128)S(1)}, f32[16,256]{1,0:T(8,128)}, u32[]{:S(2)}) copy-start(f32[16,256]{1,0:T(8,128)} %input_ref.1) | copy-start | bytes 49156
  2.0 7.8 %copy-start.9 = (f32[256]{0:T(256)S(1)}, f32[256]{0:T(256)}, u32[]{:S(2)}) copy-start(f32[256]{0:T(256)} %param.20) | copy-start | bytes 3076
  2.0 7.8 %copy-start.10 = (f32[256]{0:T(256)S(1)}, f32[256]{0:T(256)}, u32[]{:S(2)}) copy-start(f32[256]{0:T(256)} %param.14) | copy-start | bytes 3076
  2.0 7.8 %copy-start.11 = (f32[256]{0:T(256)S(1)}, f32[256]{0:T(256)}, u32[]{:S(2)}) copy-start(f32[256]{0:T(256)} %param.15) | copy-start | bytes 3076
  2.0 14.6 %all-to-all-start = ((f32[16,8,256]{2,1,0:T(8,128)}), f32[16,8,256]{2,1,0:T(8,128)S(1)}, u32[]{:S(2)}, u32[]{:S(2)}) async-start(f32[16,8,256]{2,1,0:T(8,128)} %bitcast.27), calls=%async_computation | async-start | bytes 262144 | tf_op jit(solution)/shard_map/stats/all_to_all | solution.py:455
  9.8 0.7 copy-start.3
  18.3 10.9 %all-to-all-start.1 = ((bf16[16,32,256]{2,1,0:T(8,128)(2,1)}), bf16[16,32,256]{2,1,0:T(8,128)(2,1)S(1)}, u32[]{:S(2)}, u32[]{:S(2)}) async-start(bf16[16,32,256]{2,1,0:T(8,128)(2,1)} %bitcast.6), calls=%async_computation.1 | async-start | bytes 524288 | tf_op jit(solution)/shard_map/local/all_to_all | solution.py:489
  21.9 7.3 %copy-start = (bf16[256,1024]{1,0:T(8,128)(2,1)S(1)}, bf16[256,1024]{1,0:T(8,128)(2,1)}, u32[]{:S(2)}) copy-start(bf16[256,1024]{1,0:T(8,128)(2,1)} %weight_ref.5) | copy-start | bytes 1572868
  30.2 4.4 %collective-permute-start = (bf16[128,1024]{1,0:T(8,128)(2,1)S(1)}, bf16[128,1024]{1,0:T(8,128)(2,1)S(1)}, u32[]{:S(2)}, u32[]{:S(2)}) collective-permute-start(bf16[128,1024]{1,0:T(8,128)(2,1)S(1)} %get-tuple-element.31), channel_id=1, source_target_pairs={{0,1},{1,0},{2,3},{3,2},{4,5},{5,4},{6,7},{7,6},{8,9},{9,8},{10,11... | collective-permute-start | bytes 786440 | tf_op jit(solution)/shard_map/shared/ppermute | solution.py:508
  34.7 19.1 %copy-start.2 = (f32[1024]{0:T(1024)S(1)}, f32[1024]{0:T(1024)}, u32[]{:S(2)}) copy-start(f32[1024]{0:T(1024)} %param.22) | copy-start | bytes 12292
  53.8 15.5 %copy-start.4 = (bf16[1024,256]{1,0:T(8,128)(2,1)S(1)}, bf16[1024,256]{1,0:T(8,128)(2,1)}, u32[]{:S(2)}) copy-start(bf16[1024,256]{1,0:T(8,128)(2,1)} %weight_ref.7) | copy-start | bytes 1572868
  66.1 4.3 %collective-permute-start.1 = (bf16[128,1024]{1,0:T(8,128)(2,1)S(1)}, bf16[128,1024]{1,0:T(8,128)(2,1)S(1)}, u32[]{:S(2)}, u32[]{:S(2)}) collective-permute-start(bf16[128,1024]{1,0:T(8,128)(2,1)S(1)} %bitcast.18), channel_id=1, source_target_pairs={{0,1},{1,0},{2,3},{3,2},{4,5},{5,4},{6,7},{7,6},{8,9},{9,8},{10,11... | collective-permute-start | bytes 786440 | tf_op jit(solution)/shard_map/output/ppermute | solution.py:522

commit v7 on v6

--- a/solution.py
+++ b/solution.py
@@ -314,7 +314,7 @@
     power_ref,
     weight_ref,
     give_ref,
-    active_ref,
+    keep_ref,
     entering,
     mixed,
 ):
@@ -361,19 +361,13 @@
     retained = retained_ref[...]
     ema = jnp.concatenate([retained, retained], axis=1) * mixed[...]
     active = (ema / (1.0 + jnp.exp(-ema))).astype(bf16)
-    active_ref[...] = active
-    give_ref[...] = half_product(1 - core, active, weight_ref[...])
-
-
-def half_product(side, active, weight):
-    wanted = iota2((HALF, LENGTH), 0) + side * HALF
-    chosen = as_bf16(time_of(iota2((HALF, LENGTH), 1)) == wanted)
-    return dot(dot(chosen, active).astype(bf16), weight).astype(bf16)
-
-
-def keep_kernel(active_ref, weight_ref, keep_ref):
-    core = lax.axis_index("tensor") % 2
-    keep_ref[...] = half_product(core, active_ref[...], weight_ref[...])
+    slot = iota2((LENGTH, LENGTH), 0)
+    wanted = (slot + (1 - core) * HALF) % LENGTH
+    chosen = as_bf16(time_of(iota2((LENGTH, LENGTH), 1)) == wanted)
+    ordered = dot(chosen, active).astype(bf16)
+    product = dot(ordered, weight_ref[...]).astype(bf16)
+    give_ref[...] = product[:HALF]
+    keep_ref[...] = product[HALF:]
 
 
 def norm_kernel(parts_ref, gain_ref, out_ref):
@@ -496,23 +490,16 @@
         )(scaled, ends, retained, pack)
     with jax.named_scope("finish"):
         width = shared_weight.shape[1]
-        give, active = call(
+        give, keep = call(
             finish_kernel,
             8,
-            [((HALF, width), bf16), ((LENGTH, WIDTH), bf16)],
+            [((HALF, width), bf16), ((HALF, width), bf16)],
             [pltpu.VMEM((32, WIDTH), f32), pltpu.VMEM((LENGTH, WIDTH), f32)],
             limit=16,
         )(message, stats, mixed, retained, pack, enter, power, shared_weight)
     with jax.named_scope("shared"):
         swap = [(i, i ^ 1) for i in range(16)]
         taken = lax.ppermute(give, "tensor", swap)
-        keep = call(
-            keep_kernel,
-            2,
-            [((HALF, width), bf16)],
-            limit=16,
-            cost=pl.CostEstimate(flops=10**9, bytes_accessed=2**20, transcendentals=0),
-        )(active, shared_weight)
         pair = (taken.astype(f32) + keep.astype(f32)).astype(bf16)
         groups = [[core + 2 * z for z in range(8)] for core in range(2)]
         parts = lax.all_to_all(pair, "tensor", 0, 0, tiled=True, axis_index_groups=groups)

time: 71.8 us -> 71.8 us (level)
  no operation moved by 1% of the time
where the time goes in v7:
time: 71.8 us; the launch traced here: 71.4 us
  blocking collectives  31.3 us (44%)
  starting transfers between devices  17.7 us (25%)
  waiting for transfers between devices  11.9 us (17%)
  Pallas kernels  9.66 us (13%)
    all_to_all x1, blocking collectives, shards(): lax.all_to_all(pair, 'tensor', 0, 0, tiled=True, axis_index_groups=groups)  19.1 us
    all_to_all x1, blocking collectives, shards(): lax.all_to_all(copies, 'tensor', 0, 0, tiled=True, axis_index_groups=groups)  12.2 us
    all_to_all x1, starting transfers between devices, shards(): stats = lax.all_to_all(own, 'span', 0, 0, tiled=True)  7.73 us
    all_to_all x1, waiting for transfers between devices, shards(): stats = lax.all_to_all(own, 'span', 0, 0, tiled=True)  5.3 us
    all_to_all x1, waiting for transfers between devices, shards(): message = lax.all_to_all(message, 'span', 0, 0, tiled=True)  5.11 us
    all_to_all x1, starting transfers between devices, shards(): message = lax.all_to_all(message, 'span', 0, 0, tiled=True)  3.53 us
    ppermute x1, starting transfers between devices, shards(): taken = lax.ppermute(give, 'tensor', swap)  3.23 us
    ppermute x1, starting transfers between devices, shards(): other = lax.ppermute(half, 'tensor', swap)  3.17 us
  transfers between devices with their start and end apart: 4, of which 4 were waited for; matrix products, arithmetic and copies ran while one was open for 0% of the time, Pallas kernels for 6%

profile of v7, /device:TPU:1, one launch (start us, length us, event | category | flops | bytes accessed | tf_op | source)
XLA Modules:
  0.0 71.4 jit_solution(11114431056105654438)
XLA Ops:
  0.0 1.9 %stats.1 = f32[128,256]{1,0:T(8,128)} custom-call(bf16[256,256]{1,0:T(8,128)(2,1)} %tokens_ref.1, f32[1,256]{1,0:T(1,128)} %bitcast.21), custom_call_target="tpu_custom_call" | custom-call | tf_op jit(solution)/shard_map/stats/pallas_call | solution.py:437
  2.0 0.0 copy-start.6
  2.0 0.0 copy-start.7
  2.0 0.0 copy-start.9
  2.0 0.0 copy-start.10
  2.0 7.7 %all-to-all-start = ((f32[16,8,256]{2,1,0:T(8,128)}), f32[16,8,256]{2,1,0:T(8,128)S(1)}, u32[]{:S(2)}, u32[]{:S(2)}) async-start(f32[16,8,256]{2,1,0:T(8,128)} %bitcast.27), calls=%async_computation | async-start | bytes 262144 | tf_op jit(solution)/shard_map/stats/all_to_all | solution.py:449
  9.9 0.6 copy-done.3
  10.5 0.9 %local.3 = (f32[256,256]{1,0:T(8,128)S(1)}, f32[256,256]{1,0:T(8,128)S(1)}, f32[256,256]{1,0:T(8,128)S(1)}, f32[256,128]{1,0:T(8,128)S(1)}, f32[256,128]{1,0:T(8...) custom-call(bf16[256,256]{1,0:T(8,128)(2,1)S(1)} %copy-done.1, ...), custom_call_target="tpu_custom_call" | custom-call | flops 2000000000 | bytes 4194304 | tf_op jit(solution)/shard_map/local/pallas_call | solution.py:451
  11.3 5.3 %all-to-all-done = f32[16,8,256]{2,1,0:T(8,128)S(1)} async-done(((f32[16,8,256]{2,1,0:T(8,128)}), f32[16,8,256]{2,1,0:T(8,128)S(1)}, u32[]{:S(2)}, u32[]{:S(2)}) %all-to-all-start) | async-done | bytes 131104 | tf_op jit(solution)/shard_map/stats/all_to_all | solution.py:449
  16.6 1.7 %local.4 = (bf16[512,256]{1,0:T(8,128)(2,1)}, f32[256,256]{1,0:T(8,128)S(1)}, f32[256,256]{1,0:T(8,128)S(1)}) custom-call(f32[128,256]{1,0:T(8,128)S(1)} %bitcast.13, f32[256,256]{1,0:T(8,128)S(1)} %get-tuple-element.19.sums_ref, f32[256,256]{1,0:T(8,128)S(1)} %get-tuple-element.20.squares_ref, f32[256,256]{1,0:T(8,128)S(1)} %get-tuple-element.21.placed_ref, ...), custom_call_target="tpu_custom_call" | custom-call | tf_op jit(solution)/shard_map/local/pallas_call | solution.py:472
  18.3 3.5 %all-to-all-start.1 = ((bf16[16,32,256]{2,1,0:T(8,128)(2,1)}), bf16[16,32,256]{2,1,0:T(8,128)(2,1)S(1)}, u32[]{:S(2)}, u32[]{:S(2)}) async-start(bf16[16,32,256]{2,1,0:T(8,128)(2,1)} %bitcast.6), calls=%async_computation.1 | async-start | bytes 524288 | tf_op jit(solution)/shard_map/local/all_to_all | solution.py:483
  21.9 2.2 %local.5.mixed_ref = f32[256,256]{1,0:T(8,128)S(1)} custom-call(f32[256,256]{1,0:T(8,128)S(1)} %get-tuple-element.27.scaled_ref, f32[256,256]{1,0:T(8,128)S(1)} %get-tuple-element.28.ends_ref, f32[256,128]{1,0:T(8,128)S(1)} %get-tuple-element.29.retained_ref, f32[216,256]{1,0:T(8,128)S(1)} %get-tuple-element.23.pack_ref), custom_call_target="tpu_custom_call" | custom-call | flops 2000000000 | bytes 4194304 | tf_op jit(solution)/shard_map/local/pallas_call | solution.py:484
  24.1 5.1 %all-to-all-done.1 = bf16[16,32,256]{2,1,0:T(8,128)(2,1)S(1)} async-done(((bf16[16,32,256]{2,1,0:T(8,128)(2,1)}), bf16[16,32,256]{2,1,0:T(8,128)(2,1)S(1)}, u32[]{:S(2)}, u32[]{:S(2)}) %all-to-all-start.1) | async-done | bytes 262176 | tf_op jit(solution)/shard_map/local/all_to_all | solution.py:483
  29.2 1.1 %finish.1 = (bf16[128,1024]{1,0:T(8,128)(2,1)S(1)}, bf16[128,1024]{1,0:T(8,128)(2,1)S(1)}) custom-call(bf16[512,256]{1,0:T(8,128)(2,1)S(1)} %bitcast.17, f32[128,256]{1,0:T(8,128)S(1)} %bitcast.14, f32[256,256]{1,0:T(8,128)S(1)} %local.5.mixed_ref, f32[256,128]{1,0:T(8,128)S(1)} %get-tuple-element.29.retained_ref, ...), custom_call_target="tpu_custom_call" | custom-call | tf_op jit(solution)/shard_map/finish/pallas_call | solution.py:493
  30.3 3.2 %collective-permute-start = (bf16[128,1024]{1,0:T(8,128)(2,1)S(1)}, bf16[128,1024]{1,0:T(8,128)(2,1)S(1)}, u32[]{:S(2)}, u32[]{:S(2)}) collective-permute-start(bf16[128,1024]{1,0:T(8,128)(2,1)S(1)} %get-tuple-element.31), channel_id=1, source_target_pairs={{0,1},{1,0},{2,3},{3,2},{4,5},{5,4},{6,7},{7,6},{8,9},{9,8},{10,11... | collective-permute-start | bytes 786440 | tf_op jit(solution)/shard_map/shared/ppermute | solution.py:502
  33.5 1.2 %collective-permute-done = bf16[128,1024]{1,0:T(8,128)(2,1)S(1)} collective-permute-done((bf16[128,1024]{1,0:T(8,128)(2,1)S(1)}, bf16[128,1024]{1,0:T(8,128)(2,1)S(1)}, u32[]{:S(2)}, u32[]{:S(2)}) %collective-permute-start) | collective-permute-done | bytes 262176 | tf_op jit(solution)/shard_map/shared/ppermute | solution.py:502
  34.7 0.1 add_convert_fusion
  34.8 19.1 %all_to_all.44 = bf16[8,16,1024]{2,1,0:T(8,128)(2,1)S(1)} all-to-all(bf16[8,16,1024]{2,1,0:T(8,128)(2,1)S(1)} %bitcast.26), channel_id=1, replica_groups={{0,2,4,6,8,10,12,14},{1,3,5,7,9,11,13,15},{16,18,20,22,24,26,28,30},{17..., dimensions={0} | all-to-all | bytes 524288 | tf_op jit(solution)/shard_map/shared/all_to_all | solution.py:505
  53.8 0.1 shared.1
  54.0 12.2 %all_to_all.45 = bf16[8,16,1024]{2,1,0:T(8,128)(2,1)S(1)} all-to-all(bf16[8,16,1024]{2,1,0:T(8,128)(2,1)S(1)} %bitcast.16), channel_id=1, replica_groups={{0,2,4,6,8,10,12,14},{1,3,5,7,9,11,13,15},{16,18,20,22,24,26,28,30},{17..., dimensions={0} | all-to-all | bytes 524288 | tf_op jit(solution)/shard_map/output/all_to_all | solution.py:508
  66.2 3.2 %collective-permute-start.1 = (bf16[128,1024]{1,0:T(8,128)(2,1)S(1)}, bf16[128,1024]{1,0:T(8,128)(2,1)S(1)}, u32[]{:S(2)}, u32[]{:S(2)}) collective-permute-start(bf16[128,1024]{1,0:T(8,128)(2,1)S(1)} %bitcast.18), channel_id=1, source_target_pairs={{0,1},{1,0},{2,3},{3,2},{4,5},{5,4},{6,7},{7,6},{8,9},{9,8},{10,11... | collective-permute-start | bytes 786440 | tf_op jit(solution)/shard_map/output/ppermute | solution.py:509
  69.3 0.9 %output.2.refs_0_ = bf16[256,256]{1,0:T(8,128)(2,1)} custom-call(bf16[128,1024]{1,0:T(8,128)(2,1)S(1)} %bitcast.19, bf16[1024,256]{1,0:T(8,128)(2,1)S(1)} %copy-done.4), custom_call_target="tpu_custom_call" | custom-call | flops 1000000000 | bytes 1048576 | tf_op jit(solution)/shard_map/output/pallas_call | solution.py:395
  70.2 0.3 collective-permute-done.1.shared_ref
  70.5 0.9 %output.3 = bf16[256,256]{1,0:T(8,128)(2,1)} custom-call(bf16[128,1024]{1,0:T(8,128)(2,1)S(1)} %collective-permute-done.1.shared_ref, bf16[1024,256]{1,0:T(8,128)(2,1)S(1)} %copy-done.4, bf16[256,256]{1,0:T(8,128)(2,1)} %output.2.refs_0_), custom_call_target="tpu_custom_call", output_to_operand_aliasing={{}: (2, {})} | custom-call | flops 1000000000 | bytes 1048576 | tf_op jit(solution)/shard_map/output/pallas_call | solution.py:395
  (19 shorter events, 0.1 us)
Async XLA Ops:
  1.9 7.8 %copy-start.1 = (bf16[256,256]{1,0:T(8,128)(2,1)S(1)}, bf16[256,256]{1,0:T(8,128)(2,1)}, u32[]{:S(2)}) copy-start(bf16[256,256]{1,0:T(8,128)(2,1)} %tokens_ref.1) | copy-start | bytes 393220
  2.0 7.8 %copy-start.5 = (f32[2,16,256]{2,1,0:T(8,128)S(1)}, f32[2,16,256]{2,1,0:T(8,128)}, u32[]{:S(2)}) copy-start(f32[2,16,256]{2,1,0:T(8,128)} %output_ref.1) | copy-start | bytes 98308
  2.0 7.8 %copy-start.6 = (f32[16,256]{1,0:T(8,128)S(1)}, f32[16,256]{1,0:T(8,128)}, u32[]{:S(2)}) copy-start(f32[16,256]{1,0:T(8,128)} %decay_ref.1) | copy-start | bytes 49156
  2.0 7.8 %copy-start.7 = (f32[16,256]{1,0:T(8,128)S(1)}, f32[16,256]{1,0:T(8,128)}, u32[]{:S(2)}) copy-start(f32[16,256]{1,0:T(8,128)} %angle_ref.1) | copy-start | bytes 49156
  2.0 7.8 %copy-start.8 = (f32[16,256]{1,0:T(8,128)S(1)}, f32[16,256]{1,0:T(8,128)}, u32[]{:S(2)}) copy-start(f32[16,256]{1,0:T(8,128)} %input_ref.1) | copy-start | bytes 49156
  2.0 7.8 %copy-start.9 = (f32[256]{0:T(256)S(1)}, f32[256]{0:T(256)}, u32[]{:S(2)}) copy-start(f32[256]{0:T(256)} %param.20) | copy-start | bytes 3076
  2.0 7.8 %copy-start.10 = (f32[256]{0:T(256)S(1)}, f32[256]{0:T(256)}, u32[]{:S(2)}) copy-start(f32[256]{0:T(256)} %param.14) | copy-start | bytes 3076
  2.0 7.8 %copy-start.11 = (f32[256]{0:T(256)S(1)}, f32[256]{0:T(256)}, u32[]{:S(2)}) copy-start(f32[256]{0:T(256)} %param.15) | copy-start | bytes 3076
  2.0 14.6 %all-to-all-start = ((f32[16,8,256]{2,1,0:T(8,128)}), f32[16,8,256]{2,1,0:T(8,128)S(1)}, u32[]{:S(2)}, u32[]{:S(2)}) async-start(f32[16,8,256]{2,1,0:T(8,128)} %bitcast.27), calls=%async_computation | async-start | bytes 262144 | tf_op jit(solution)/shard_map/stats/all_to_all | solution.py:449
  9.8 0.7 copy-start.3
  18.3 10.9 %all-to-all-start.1 = ((bf16[16,32,256]{2,1,0:T(8,128)(2,1)}), bf16[16,32,256]{2,1,0:T(8,128)(2,1)S(1)}, u32[]{:S(2)}, u32[]{:S(2)}) async-start(bf16[16,32,256]{2,1,0:T(8,128)(2,1)} %bitcast.6), calls=%async_computation.1 | async-start | bytes 524288 | tf_op jit(solution)/shard_map/local/all_to_all | solution.py:483
  21.9 7.3 %copy-start = (bf16[256,1024]{1,0:T(8,128)(2,1)S(1)}, bf16[256,1024]{1,0:T(8,128)(2,1)}, u32[]{:S(2)}) copy-start(bf16[256,1024]{1,0:T(8,128)(2,1)} %weight_ref.3) | copy-start | bytes 1572868
  30.3 4.4 %collective-permute-start = (bf16[128,1024]{1,0:T(8,128)(2,1)S(1)}, bf16[128,1024]{1,0:T(8,128)(2,1)S(1)}, u32[]{:S(2)}, u32[]{:S(2)}) collective-permute-start(bf16[128,1024]{1,0:T(8,128)(2,1)S(1)} %get-tuple-element.31), channel_id=1, source_target_pairs={{0,1},{1,0},{2,3},{3,2},{4,5},{5,4},{6,7},{7,6},{8,9},{9,8},{10,11... | collective-permute-start | bytes 786440 | tf_op jit(solution)/shard_map/shared/ppermute | solution.py:502
  34.7 19.1 %copy-start.2 = (f32[1024]{0:T(1024)S(1)}, f32[1024]{0:T(1024)}, u32[]{:S(2)}) copy-start(f32[1024]{0:T(1024)} %param.22) | copy-start | bytes 12292
  53.8 15.5 %copy-start.4 = (bf16[1024,256]{1,0:T(8,128)(2,1)S(1)}, bf16[1024,256]{1,0:T(8,128)(2,1)}, u32[]{:S(2)}) copy-start(bf16[1024,256]{1,0:T(8,128)(2,1)} %weight_ref.5) | copy-start | bytes 1572868
  66.2 4.3 %collective-permute-start.1 = (bf16[128,1024]{1,0:T(8,128)(2,1)S(1)}, bf16[128,1024]{1,0:T(8,128)(2,1)S(1)}, u32[]{:S(2)}, u32[]{:S(2)}) collective-permute-start(bf16[128,1024]{1,0:T(8,128)(2,1)S(1)} %bitcast.18), channel_id=1, source_target_pairs={{0,1},{1,0},{2,3},{3,2},{4,5},{5,4},{6,7},{7,6},{8,9},{9,8},{10,11... | collective-permute-start | bytes 786440 | tf_op jit(solution)/shard_map/output/ppermute | solution.py:509
